TPU v7x, 32 devices: a whole 2x2x4 slice. The times are simulated.
32 devices in a mesh: row: 4 (over y, core), col: 8 (over z, x).
Axes of the slice: x: 2, y: 2, z: 4, core: 2. Of those that a mesh axis runs over, the one named last changes fastest.
Arguments:
- embedding: bfloat16 [512, 128], P('row'), may hold values from -6 to 6
- kernel: bfloat16 [3, 3, 64, 64], replicated, may hold values from -0.25 to 0.25
- cotangent: bfloat16 [512, 512, 64], P('row', 'col'), may hold values from -6 to 6
Outputs:
- prediction: float32 [512, 512, 64], P('row', 'col')
- grad_kernel: float32 [3, 3, 64, 64], replicated
- grad_embedding: float32 [512, 128], P('row')
All inputs are finite; a program needn't handle non-finite values.
Results may differ from a plain program's by a relative error of at most 0.0031.
Values may be sent and summed in bfloat16 or wider, within the bound.
A program may use at most 128 MiB of HBM per device.

v0:
```python
import jax
import jax.numpy as jnp
from jax import lax
from jax.sharding import PartitionSpec as P

DILATION_STEP = 8


def from_root(shard, axis, root):
    mine = lax.axis_index(axis) == root
    return lax.psum(jnp.where(mine, shard, jnp.zeros_like(shard)), axis)


def padded(cells, sides, width):
    for axis, dim in sides:
        count = lax.axis_size(axis)
        ends = count - 1
        head = lax.slice_in_dim(cells, 0, width, axis=dim)
        tail = lax.slice_in_dim(cells, cells.shape[dim] - width, cells.shape[dim], axis=dim)
        cells = jnp.concatenate(
            [
                lax.ppermute(tail, axis, [(i, (i + 1) % count) for i in range(ends)]),
                cells,
                lax.ppermute(head, axis, [((i + 1) % count, i) for i in range(ends)]),
            ],
            axis=dim,
        )
    return cells


def build_pairs(row_embedding, col_embed, channels):
    return (
        row_embedding[:, None, :channels] * col_embed[None, :, :channels]
        + row_embedding[:, None, channels:]
        + col_embed[None, :, channels:]
    )


def on_device(embedding, kernel, cotangent):
    rows_local = embedding.shape[0]
    columns_local = cotangent.shape[1]
    channels = kernel.shape[2]
    col_ratio = lax.axis_size("col") // lax.axis_size("row")
    bin_count = rows_local * lax.axis_size("row")
    row_id = lax.axis_index("row")
    col_id = lax.axis_index("col")
    own_slice = lax.dynamic_slice_in_dim(
        embedding, col_id % col_ratio * columns_local, columns_local, 0
    )
    col_embed = from_root(own_slice, "row", col_id // col_ratio)
    row_float = embedding.astype(jnp.float32)
    col_float = col_embed.astype(jnp.float32)
    row_wide = padded(embedding, (("row", 0),), DILATION_STEP).astype(jnp.float32)
    col_wide = padded(col_embed, (("col", 0),), DILATION_STEP).astype(jnp.float32)
    row_pos = (
        row_id * rows_local
        - DILATION_STEP
        + jnp.arange(rows_local + 2 * DILATION_STEP, dtype=jnp.int32)
    )
    col_pos = (
        col_id * columns_local
        - DILATION_STEP
        + jnp.arange(columns_local + 2 * DILATION_STEP, dtype=jnp.int32)
    )
    row_valid = ((row_pos >= 0) & (row_pos < bin_count)).astype(jnp.float32)
    col_valid = ((col_pos >= 0) & (col_pos < bin_count)).astype(jnp.float32)
    valid_wide = row_valid[:, None, None] * col_valid[None, :, None]
    wide_pre = build_pairs(row_wide, col_wide, channels)
    activation_wide = (jax.nn.silu(wide_pre) * valid_wide).astype(jnp.bfloat16)
    preactivation = wide_pre[
        DILATION_STEP : DILATION_STEP + rows_local, DILATION_STEP : DILATION_STEP + columns_local
    ]
    cotangent_wide = padded(cotangent, (("row", 0), ("col", 1)), DILATION_STEP)
    forward = jnp.zeros((rows_local, columns_local, channels), jnp.float32)
    backward = jnp.zeros((rows_local, columns_local, channels), jnp.float32)
    kernel_rows = []
    for kernel_tap_row in range(3):
        kernel_cols = []
        for kernel_tap_column in range(3):
            shifted_pairs = activation_wide[
                kernel_tap_row * DILATION_STEP : kernel_tap_row * DILATION_STEP + rows_local,
                kernel_tap_column * DILATION_STEP : kernel_tap_column * DILATION_STEP
                + columns_local,
            ]
            forward = forward + jnp.einsum(
                "ijc,cd->ijd",
                shifted_pairs,
                kernel[kernel_tap_row, kernel_tap_column],
                preferred_element_type=jnp.float32,
            )
            kernel_cols.append(
                jnp.einsum(
                    "ijc,ijd->cd", shifted_pairs, cotangent, preferred_element_type=jnp.float32
                )
            )
            cotangent_shifted = cotangent_wide[
                (2 - kernel_tap_row) * DILATION_STEP : (2 - kernel_tap_row) * DILATION_STEP
                + rows_local,
                (2 - kernel_tap_column) * DILATION_STEP : (2 - kernel_tap_column) * DILATION_STEP
                + columns_local,
            ]
            backward = backward + jnp.einsum(
                "ijd,cd->ijc",
                cotangent_shifted,
                kernel[kernel_tap_row, kernel_tap_column],
                preferred_element_type=jnp.float32,
            )
        kernel_rows.append(jnp.stack(kernel_cols))
    kernel_local = jnp.stack(kernel_rows)
    sigmoid_val = jax.nn.sigmoid(preactivation)
    grad_pre = backward * sigmoid_val * (1.0 + preactivation * (1.0 - sigmoid_val))
    row_part = jnp.concatenate(
        [jnp.sum(grad_pre * col_float[None, :, :channels], axis=1), jnp.sum(grad_pre, axis=1)],
        axis=1,
    )
    col_part = jnp.concatenate(
        [jnp.sum(grad_pre * row_float[:, None, :channels], axis=0), jnp.sum(grad_pre, axis=0)],
        axis=1,
    )
    kernel_total = lax.psum(kernel_local, ("row", "col"))
    row_total = lax.psum(row_part, "col")
    col_total = lax.psum(col_part, "row")
    pieces = []
    for part_index in range(col_ratio):
        pieces.append(from_root(col_total, "col", row_id * col_ratio + part_index))
    col_full = jnp.concatenate(pieces, axis=0)
    grad_kernel = kernel_total / bin_count
    grad_embedding = (row_total + col_full) * float(bin_count) ** (-0.5)
    return (forward, grad_kernel, grad_embedding)


def solution(mesh):
    in_specs = (P("row", None), P(), P("row", "col", None))
    out_specs = (P("row", "col", None), P(), P("row", None))
    return jax.shard_map(
        on_device, mesh=mesh, in_specs=in_specs, out_specs=out_specs, check_vma=False
    )
```

profile of v0, /device:TPU:0, one launch (start us, length us, event | category | flops | bytes accessed | tf_op | source)
XLA Modules:
  0.0 349.3 jit_solution(10809640441525689311)
XLA Ops:
  7.2 0.7 dynamic-slice_select_fusion
  8.0 12.7 %psum.42 = bf16[64,128]{1,0:T(8,128)(2,1)S(1)} all-reduce(bf16[64,128]{1,0:T(8,128)(2,1)S(1)} %dynamic-slice_select_fusion), channel_id=1, replica_groups=mesh['row'=4,'col'=8] {'row'}, use_global_device_ids=true, to_apply=%region_0.1 | all-reduce | flops 8192 | bytes 32768 | tf_op jit(solution)/shard_map/psum | solution.py:11
  20.6 3.4 collective-permute-start.2
  24.0 1.3 collective-permute-start.3
  25.3 0.7 fusion.87
  26.0 1.3 collective-permute-start
  27.3 1.4 collective-permute-start.1
  28.8 2.1 fusion.84
  30.9 0.4 copy.142
  31.3 4.4 %collective-permute-start.4 = (bf16[8,64,64]{2,1,0:T(8,128)(2,1)S(1)}, bf16[8,64,64]{2,1,0:T(8,128)(2,1)}, u32[]{:S(2)}, u32[]{:S(2)}) collective-permute-start(bf16[8,64,64]{2,1,0:T(8,128)(2,1)S(1)} %copy.142), channel_id=1, source_target_pairs={{0,8},{8,16},{16,24},{1,9},{9,17},{17,25},{2,10},{10,18},{18,26},{... | collective-permute-start | bytes 196616 | tf_op jit(solution)/shard_map/ppermute | solution.py:22
  35.7 1.7 fusion.53
  37.6 0.4 copy.143
  38.0 0.1 copy.144
  38.1 1.3 collective-permute-start.5
  39.6 0.1 fusion.85
  39.6 0.1 copy.85
  39.8 4.2 %add_add_fusion = (f32[144,80,64]{0,2,1:T(8,128)}, bf16[144,80,64]{0,2,1:T(8,128)(2,1)S(1)}) fusion(f32[80,64]{1,0:T(8,128)S(1)} %get-tuple-element.31, f32[144,64]{0,1:T(8,128)S(1)} %copy.86, f32[80,64]{1,0:T(8,128)S(1)} %get-tuple-element.30, f32[144,64]{0,1:T(8,128)S(1)} %copy.85, f32[144,80]{0,1:T(8,128)S(1)} %broadcast_multiply_fusion.1), kind=kLoop, calls=%fused_computation.1 | loop fusion | flops 6635520 | bytes 4584448 | tf_op jit(solution)/shard_map/add | solution.py:33
  44.0 0.5 convolution_bitcast_fusion.3
  44.6 0.5 convolution_bitcast_fusion.4
  45.1 0.5 convolution_bitcast_fusion.5
  45.6 0.4 convolution_bitcast_fusion.6
  46.1 0.4 convolution_bitcast_fusion.7
  46.5 0.4 convolution_bitcast_fusion.8
  46.9 0.5 convolution_bitcast_fusion
  47.4 0.5 convolution_bitcast_fusion.1
  48.0 0.5 convolution_bitcast_fusion.2
  48.5 1.9 fusion.21
  50.4 1.9 fusion.24
  52.3 1.8 fusion.27
  54.2 2.0 fusion.30
  56.1 1.8 fusion.33
  58.0 1.8 fusion.36
  59.8 1.8 fusion.39
  61.5 1.8 fusion.42
  63.4 0.7 pad_maximum_fusion.5
  64.1 0.2 all-reduce.9.cloned.1.call-start
  64.4 8.5 %add_add_fusion.1 = f32[128,64,64]{0,2,1:T(8,128)} fusion(f32[128,64,64]{0,2,1:T(8,128)} %fusion.21, f32[128,64,64]{0,2,1:T(8,128)} %fusion.24, f32[128,64,64]{0,2,1:T(8,128)} %fusion.27, f32[128,64,64]{0,2,1:T(8,128)} %fusion.30, f32[128,64,64]{0,2,1:T(8,128)} %fusion.33, f32[128,64,64]{0,2,1:T(8,128)} %fusion.36, f32[128,64,64]{0,2,1:T(8,128)} %fusion.42, ...), kind=kOutput, calls=%fused_computation.7 | convolution fusion | flops 71303168 | bytes 19939328 | tf_op jit(solution)/shard_map/ijc,cd->ijd/dot_general | solution.py:85
  72.9 1.4 copy.99
  74.2 3.6 %fusion.14 = f32[128,64,64]{0,2,1:T(8,128)} fusion(bf16[8,64,64]{0,2,1:T(8,128)(2,1)S(1)} %copy.99, bf16[128,64,64]{0,2,1:T(8,128)(2,1)} %param.5, bf16[3,3,64,64]{3,2,1,0:T(8,128)(2,1)S(1)} %copy-done.5), kind=kOutput, calls=%fused_computation.31 | convolution fusion | flops 69206016 | bytes 4210688 | tf_op jit(solution)/shard_map/ijd,cd->ijc/dot_general | solution.py:102
  77.8 1.4 copy.98
  79.2 0.3 pad_maximum_fusion.6
  79.5 1.3 collective-permute-start.6
  80.8 5.2 %collective-permute-start.7 = (bf16[144,8,64]{0,2,1:T(8,128)(2,1)S(1)}, bf16[144,8,64]{0,2,1:T(8,128)(2,1)S(1)}, u32[]{:S(2)}, u32[]{:S(2)}) collective-permute-start(bf16[144,8,64]{0,2,1:T(8,128)(2,1)S(1)} %get-tuple-element.20), channel_id=1, source_target_pairs={{0,1},{1,2},{2,3},{3,4},{4,5},{5,6},{6,7},{8,9},{9,10},{10,11},{11... | collective-permute-start | bytes 442376 | tf_op jit(solution)/shard_map/ppermute | solution.py:22
  86.0 0.7 fusion.4
  86.8 3.6 %collective-permute-done.6 = bf16[144,8,64]{0,2,1:T(8,128)(2,1)S(1)} collective-permute-done((bf16[144,8,64]{0,2,1:T(8,128)(2,1)S(1)}, bf16[144,8,64]{0,2,1:T(8,128)(2,1)S(1)}, u32[]{:S(2)}, u32[]{:S(2)}) %collective-permute-start.6) | collective-permute-done | bytes 147488 | tf_op jit(solution)/shard_map/ppermute | solution.py:24
  90.4 7.0 %collective-permute-done.7 = bf16[144,8,64]{0,2,1:T(8,128)(2,1)S(1)} collective-permute-done((bf16[144,8,64]{0,2,1:T(8,128)(2,1)S(1)}, bf16[144,8,64]{0,2,1:T(8,128)(2,1)S(1)}, u32[]{:S(2)}, u32[]{:S(2)}) %collective-permute-start.7) | collective-permute-done | bytes 147488 | tf_op jit(solution)/shard_map/ppermute | solution.py:22
  97.3 2.9 maximum_maximum_fusion
  100.2 0.5 fusion.10
  100.8 0.5 fusion.16
  101.3 0.4 fusion.6
  101.8 0.5 fusion.12
  102.3 0.5 fusion.8
  102.9 0.5 copy-done.4
  103.3 0.8 copy-done.3
  104.1 5.0 %multiply_reduce_fusion = (f32[64,64]{1,0:T(8,128)S(1)}, f32[64,64]{1,0:T(8,128)S(1)}, f32[128,64]{0,1:T(8,128)S(1)}, f32[128,64]{0,1:T(8,128)S(1)}) fusion(f32[128,64]{0,1:T(8,128)S(1)} %slice.188, f32[64,64]{1,0:T(8,128)S(1)} %slice_convert_fusion, f32[144,80,64]{0,2,1:T(8,128)} %get-tuple-element.24, bf16[144,72,64]{0,2,1:T(8,128)(2,1)S(1)} %get-tuple-element.18, ...), kind=kOutput, calls=%fused_computation.4 | convolution fusion | flops 78618624 | bytes 20103168 | tf_op jit(solution)/shard_map/ijd,cd->ijc/dot_general | solution.py:102
  109.3 12.3 %psum.45 = f32[64,128]{0,1:T(8,128)S(1)} all-reduce(f32[64,128]{0,1:T(8,128)S(1)} %pad_maximum_fusion.10), channel_id=1, replica_groups=mesh['row'=4,'col'=8] {'row'}, use_global_device_ids=true, to_apply=%region_7.8 | all-reduce | flops 8192 | bytes 65536 | tf_op jit(solution)/shard_map/psum | solution.py:122
  121.6 0.7 broadcast_select_fusion.1
  122.3 0.6 pad_maximum_fusion.9
  123.0 71.5 %all-reduce.5.cloned.1.call-done = f32[3,3,64,64]{3,2,1,0:T(8,128)} async-done(((f32[3,3,64,64]{3,2,1,0:T(8,128)}), f32[3,3,64,64]{3,2,1,0:T(8,128)}) %all-reduce.5.cloned.1.call-update) | async-done | bytes 147472 | tf_op jit(solution)/shard_map/psum | solution.py:120
  194.5 1.7 broadcast_multiply_fusion
  196.2 73.0 %all-reduce.9.cloned.1.call-done = (f32[64,128]{0,1:T(8,128)}, f32[64,128]{0,1:T(8,128)}) async-done(((f32[64,128]{0,1:T(8,128)}, f32[64,128]{0,1:T(8,128)}), (f32[64,128]{0,1:T(8,128)}, f32[64,128]{0,1:T(8,128)})) %all-reduce.9.cloned.1.call-update) | async-done | bytes 65552 | tf_op jit(solution)/shard_map/psum | solution.py:11
  269.2 71.8 %all-reduce.7.cloned.1.call-done = f32[128,128]{0,1:T(8,128)} async-done(((f32[128,128]{0,1:T(8,128)}), f32[128,128]{0,1:T(8,128)}) %all-reduce.7.cloned.1.call-update) | async-done | bytes 65552 | tf_op jit(solution)/shard_map/psum | solution.py:121
  341.0 1.0 fusion.44
  342.0 0.7 copy.114
  (38 shorter events, 0.7 us)
Async XLA Ops:
  7.2 187.3 %all-reduce.5.cloned.1.call-start = ((), (), s32[]{:S(2)}) async-start(), calls=%async_computation | async-start | bytes 589824 | tf_op jit(solution)/shard_map/psum | solution.py:120
  20.6 17.5 %collective-permute-start.2 = (bf16[8,128]{1,0:T(8,128)(2,1)S(1)}, bf16[8,128]{1,0:T(8,128)(2,1)S(1)}, u32[]{:S(2)}, u32[]{:S(2)}) collective-permute-start(bf16[8,128]{1,0:T(8,128)(2,1)S(1)} %get-tuple-element.34), channel_id=1, source_target_pairs={{0,1},{1,2},{2,3},{3,4},{4,5},{5,6},{6,7},{8,9},{9,10},{10,11},{11... | collective-permute-start | bytes 6152 | tf_op jit(solution)/shard_map/ppermute | solution.py:22
  24.0 15.4 %collective-permute-start.3 = (bf16[8,128]{1,0:T(8,128)(2,1)S(1)}, bf16[8,128]{1,0:T(8,128)(2,1)S(1)}, u32[]{:S(2)}, u32[]{:S(2)}) collective-permute-start(bf16[8,128]{1,0:T(8,128)(2,1)S(1)} %get-tuple-element.35), channel_id=1, source_target_pairs={{1,0},{2,1},{3,2},{4,3},{5,4},{6,5},{7,6},{9,8},{10,9},{11,10},{12... | collective-permute-start | bytes 6152 | tf_op jit(solution)/shard_map/ppermute | solution.py:24
  26.0 13.5 %collective-permute-start = (bf16[8,128]{1,0:T(8,128)(2,1)S(1)}, bf16[8,128]{1,0:T(8,128)(2,1)S(1)}, u32[]{:S(2)}, u32[]{:S(2)}) collective-permute-start(bf16[8,128]{1,0:T(8,128)(2,1)S(1)} %get-tuple-element.32), channel_id=1, source_target_pairs={{0,8},{8,16},{16,24},{1,9},{9,17},{17,25},{2,10},{10,18},{18,26},{... | collective-permute-start | bytes 6152 | tf_op jit(solution)/shard_map/ppermute | solution.py:22
  27.3 8.4 %copy-start = (bf16[128,64,64]{0,2,1:T(8,128)(2,1)S(1)}, bf16[128,64,64]{0,2,1:T(8,128)(2,1)}, u32[]{:S(2)}) copy-start(bf16[128,64,64]{0,2,1:T(8,128)(2,1)} %param.5) | copy-start | bytes 3145732
  27.3 8.4 %copy-start.5 = (bf16[3,3,64,64]{3,2,1,0:T(8,128)(2,1)S(1)}, bf16[3,3,64,64]{3,2,1,0:T(8,128)(2,1)}, u32[]{:S(2)}) copy-start(bf16[3,3,64,64]{3,2,1,0:T(8,128)(2,1)} %param.4) | copy-start | bytes 221188
  27.3 12.2 %collective-permute-start.1 = (bf16[8,128]{1,0:T(8,128)(2,1)S(1)}, bf16[8,128]{1,0:T(8,128)(2,1)S(1)}, u32[]{:S(2)}, u32[]{:S(2)}) collective-permute-start(bf16[8,128]{1,0:T(8,128)(2,1)S(1)} %get-tuple-element.33), channel_id=1, source_target_pairs={{8,0},{16,8},{24,16},{9,1},{17,9},{25,17},{10,2},{18,10},{26,18},{... | collective-permute-start | bytes 6152 | tf_op jit(solution)/shard_map/ppermute | solution.py:24
  31.3 6.7 %copy-start.6 = (bf16[128,128]{1,0:T(8,128)(2,1)S(1)}, bf16[128,128]{1,0:T(8,128)(2,1)}, u32[]{:S(2)}) copy-start(bf16[128,128]{1,0:T(8,128)(2,1)} %param.3) | copy-start | bytes 98308
  31.3 46.5 %collective-permute-start.4 = (bf16[8,64,64]{2,1,0:T(8,128)(2,1)S(1)}, bf16[8,64,64]{2,1,0:T(8,128)(2,1)}, u32[]{:S(2)}, u32[]{:S(2)}) collective-permute-start(bf16[8,64,64]{2,1,0:T(8,128)(2,1)S(1)} %copy.142), channel_id=1, source_target_pairs={{0,8},{8,16},{16,24},{1,9},{9,17},{17,25},{2,10},{10,18},{18,26},{... | collective-permute-start | bytes 196616 | tf_op jit(solution)/shard_map/ppermute | solution.py:22
  38.1 34.7 %collective-permute-start.5 = (bf16[8,64,64]{2,1,0:T(8,128)(2,1)S(1)}, bf16[8,64,64]{2,1,0:T(8,128)(2,1)}, u32[]{:S(2)}, u32[]{:S(2)}) collective-permute-start(bf16[8,64,64]{2,1,0:T(8,128)(2,1)S(1)} %copy.143), channel_id=1, source_target_pairs={{8,0},{16,8},{24,16},{9,1},{17,9},{25,17},{10,2},{18,10},{26,18},{... | collective-permute-start | bytes 196616 | tf_op jit(solution)/shard_map/ppermute | solution.py:24
  39.8 4.2 %copy-start.1 = (bf16[128,64,64]{0,2,1:T(8,128)(2,1)S(1)}, bf16[128,64,64]{0,2,1:T(8,128)(2,1)}, u32[]{:S(2)}) copy-start(bf16[128,64,64]{0,2,1:T(8,128)(2,1)} %param.5) | copy-start | bytes 3145732
  64.1 205.1 %all-reduce.9.cloned.1.call-start = ((), (), s32[]{:S(2)}) async-start(), calls=%async_computation.2 | async-start | bytes 262144 | tf_op jit(solution)/shard_map/psum | solution.py:11
  74.2 5.0 %copy-start.2 = (bf16[128,64,64]{0,2,1:T(8,128)(2,1)S(1)}, bf16[128,64,64]{0,2,1:T(8,128)(2,1)}, u32[]{:S(2)}) copy-start(bf16[128,64,64]{0,2,1:T(8,128)(2,1)} %param.5) | copy-start | bytes 3145732
  79.5 10.8 %collective-permute-start.6 = (bf16[144,8,64]{0,2,1:T(8,128)(2,1)S(1)}, bf16[144,8,64]{0,2,1:T(8,128)(2,1)S(1)}, u32[]{:S(2)}, u32[]{:S(2)}) collective-permute-start(bf16[144,8,64]{0,2,1:T(8,128)(2,1)S(1)} %get-tuple-element.21), channel_id=1, source_target_pairs={{1,0},{2,1},{3,2},{4,3},{5,4},{6,5},{7,6},{9,8},{10,9},{11,10},{12... | collective-permute-start | bytes 442376 | tf_op jit(solution)/shard_map/ppermute | solution.py:24
  80.8 16.5 %collective-permute-start.7 = (bf16[144,8,64]{0,2,1:T(8,128)(2,1)S(1)}, bf16[144,8,64]{0,2,1:T(8,128)(2,1)S(1)}, u32[]{:S(2)}, u32[]{:S(2)}) collective-permute-start(bf16[144,8,64]{0,2,1:T(8,128)(2,1)S(1)} %get-tuple-element.20), channel_id=1, source_target_pairs={{0,1},{1,2},{2,3},{3,4},{4,5},{5,6},{6,7},{8,9},{9,10},{10,11},{11... | collective-permute-start | bytes 442376 | tf_op jit(solution)/shard_map/ppermute | solution.py:22
  101.7 1.6 copy-start.4
  102.3 1.8 copy-start.3
  122.2 218.8 %all-reduce.7.cloned.1.call-start = ((), (), s32[]{:S(2)}) async-start(), calls=%async_computation.1 | async-start | bytes 131072 | tf_op jit(solution)/shard_map/psum | solution.py:121
Sparse Core Ops, SparseCore 0:
  64.2 130.1 all-reduce.4
  198.3 70.7 all-reduce.8
  273.2 67.7 all-reduce.6
where the time goes:
time: 350 us; the launch traced here: 349 us
  waiting for transfers between devices  227 us (65%)
  matrix products  41.3 us (12%)
  blocking collectives  24.9 us (7%)
  starting transfers between devices  19.9 us (6%)
  between operations  14.2 us (4%)
  other arithmetic  13 us (4%)
  local copies, waits for them, and re-layouts  8.92 us (3%)
    psum x1, waiting for transfers between devices, from_root(): return lax.psum(jnp.where(mine, shard, jnp.zeros_like(shard)), axis)  73 us
    psum x1, waiting for transfers between devices, on_device(): row_total = lax.psum(row_part, 'col')  71.8 us
    psum x1, waiting for transfers between devices, on_device(): kernel_total = lax.psum(kernel_local, ('row', 'col'))  71.5 us
    dot_general x9, matrix products, on_device(): jnp.einsum('ijc,cd->ijd', shifted_pairs, kernel[kernel_tap_row, kernel_ta...  23.3 us
    ppermute x4, starting transfers between devices, padded(): lax.ppermute(tail, axis, [(i, (i + 1) % count) for i in range(ends)])  14.3 us
    dot_general x9, matrix products, on_device(): jnp.einsum('ijd,cd->ijc', cotangent_shifted, kernel[kernel_tap_row, kerne...  13.6 us
    psum x1, blocking collectives, from_root(): return lax.psum(jnp.where(mine, shard, jnp.zeros_like(shard)), axis)  12.7 us
    psum x1, blocking collectives, on_device(): col_total = lax.psum(col_part, 'row')  12.3 us
  transfers between devices with their start and end apart: 11, of which 5 were waited for; matrix products, arithmetic and copies ran while one was open for 17% of the time, Pallas kernels for 0%

commit v1 on v0

v1 whole, which is shorter than its diff:
```python
import functools

import jax
import jax.numpy as jnp
from jax import lax
from jax.experimental import pallas as pl
from jax.experimental.pallas import tpu as pltpu
from jax.sharding import PartitionSpec as P

STEP = 8
MESH = pl.DeviceIdType.MESH
VMEM = pl.BlockSpec(memory_space=pltpu.VMEM)
ANY = pl.BlockSpec(memory_space=pl.ANY)


def signal(barrier, row, col):
    pl.semaphore_signal(barrier, inc=1, device_id=(row, col), device_id_type=MESH)


def remote(src, dst, send, recv, row, col):
    return pltpu.make_async_remote_copy(
        src_ref=src,
        dst_ref=dst,
        send_sem=send,
        recv_sem=recv,
        device_id=(row, col),
        device_id_type=MESH,
    )


def gather_kernel(n_row, emb_ref, out_ref, held, send_sem, recv_sem):
    row, col = lax.axis_index("row"), lax.axis_index("col")
    rows = emb_ref.shape[0]
    barrier = pltpu.get_barrier_semaphore()
    peers = [lax.rem(row + d, n_row) for d in range(1, n_row)]
    for peer in peers:
        signal(barrier, peer, col)
    pl.semaphore_wait(barrier, n_row - 1)
    copies = []
    for d, peer in enumerate(peers):
        copy = remote(emb_ref, held.at[d], send_sem.at[d], recv_sem.at[d], peer, col)
        copy.start()
        copies.append(copy)
    border = jnp.zeros((STEP, out_ref.shape[1]), jnp.float32)
    out_ref[:STEP] = border
    out_ref[STEP + n_row * rows :] = border
    out_ref[pl.ds(pl.multiple_of(STEP + row * rows, STEP), rows)] = emb_ref[...].astype(jnp.float32)
    for d, copy in enumerate(copies):
        copy.wait()
        owner = lax.rem(row + n_row - 1 - d, n_row)
        out_ref[pl.ds(pl.multiple_of(STEP + owner * rows, STEP), rows)] = held[d].astype(
            jnp.float32
        )


def tile_kernel(
    n_row,
    chunk,
    wide_ref,
    kernel_ref,
    cot_hbm,
    pred_hbm,
    part_ref,
    cot_ref,
    pred_ref,
    weight_ref,
    u_row_ref,
    v_row_ref,
    act_ref,
    slope_ref,
    grad_ref,
    product_ref,
    u_sum_ref,
    v_sum_ref,
    bins_ref,
    flat_ref,
    packed_ref,
    cot_sem,
    pred_sem,
):
    rows, columns, channels = cot_ref.shape
    half = rows // 2
    blocks = half // STEP
    span = columns + 2 * STEP
    lanes = 2 * channels
    bins = n_row * rows
    row0 = lax.axis_index("row") * rows
    col0 = lax.axis_index("col") * columns

    def cot_copy(n, h):
        at = pl.ds(h * half + n * STEP, STEP)
        return pltpu.make_async_copy(cot_hbm.at[at], cot_ref.at[at], cot_sem.at[n, h])

    def pred_copy(n, h):
        at = pl.ds(h * half + n * STEP, STEP)
        return pltpu.make_async_copy(pred_ref.at[at], pred_hbm.at[at], pred_sem.at[n, h])

    for n in range(blocks):
        for h in range(2):
            cot_copy(n, h).start()

    none = jnp.zeros((channels, channels), jnp.float32)
    for a in range(3):
        for b in range(3):
            w = kernel_ref[a, b].astype(jnp.float32)
            both = jnp.concatenate(
                [jnp.concatenate([w, none], axis=1), jnp.concatenate([none, w], axis=1)], axis=0
            )
            weight_ref[a * lanes : (a + 1) * lanes, b * lanes : (b + 1) * lanes] = both.astype(
                jnp.bfloat16
            )

    def first(shape):
        return lax.broadcasted_iota(jnp.int32, shape, len(shape) - 1) < channels

    def swap(x):
        return pltpu.roll(x, channels, 1)

    depth = half + 2 * STEP
    low = wide_ref[pl.ds(pl.multiple_of(row0, STEP), depth)]
    high = wide_ref[pl.ds(pl.multiple_of(row0 + half, STEP), depth)]
    in_first = first((depth, lanes))
    u_row_ref[...] = jnp.where(in_first, low, swap(high))
    v_row_ref[...] = jnp.where(in_first, swap(low), high)
    cols = wide_ref[pl.ds(pl.multiple_of(col0, STEP), span)]
    in_first_col = first((span, lanes))
    u_col = jnp.where(in_first_col, cols, swap(cols))
    v_col = jnp.where(in_first_col, swap(cols), cols)
    col_pos = col0 - STEP + lax.broadcasted_iota(jnp.int32, (span, lanes), 0)
    col_in = jnp.where((col_pos >= 0) & (col_pos < bins), 1.0, 0.0)

    def activate(m, carry):
        at = pl.ds(pl.multiple_of(m * STEP, STEP), STEP)
        shape = (STEP, 1, lanes)
        pos = row0 - STEP + m * STEP + lax.broadcasted_iota(jnp.int32, shape, 0)
        pos = pos + jnp.where(first(shape), 0, half)
        row_in = jnp.where((pos >= 0) & (pos < bins), 1.0, 0.0)
        pairs = u_row_ref[at][:, None, :] * u_col[None] + v_row_ref[at][:, None, :] + v_col[None]
        s = 0.5 * jnp.tanh(0.5 * pairs) + 0.5
        s = s * (row_in * col_in[None])
        act = pairs * s
        act_ref[m] = act.reshape(STEP * span, lanes).astype(jnp.bfloat16)
        slope_ref[m] = s + act * (1.0 - s)
        grad_ref[m] = jnp.zeros((STEP, span, lanes), jnp.float32)
        return carry

    lax.fori_loop(0, blocks + 2, activate, 0)
    product_ref[...] = jnp.zeros_like(product_ref)

    def convolve(n, carry):
        for h in range(2):
            cot_copy(n, h).wait()
        at = [pl.ds(pl.multiple_of(h * half + n * STEP, STEP), STEP) for h in range(2)]
        x = jnp.concatenate([act_ref[n + a] for a in range(3)], axis=1)
        out = jnp.dot(x, weight_ref[...], preferred_element_type=jnp.float32)
        out = out.reshape(STEP, span, 3 * lanes)
        out = (
            out[:, :columns, :lanes]
            + out[:, STEP : STEP + columns, lanes : 2 * lanes]
            + out[:, 2 * STEP :, 2 * lanes :]
        )
        pred_ref[at[0]] = out[:, :, :channels]
        pred_ref[at[1]] = out[:, :, channels:]
        for h in range(2):
            pred_copy(n, h).start()
        cot = jnp.concatenate([cot_ref[at[h]].astype(jnp.float32) for h in range(2)], axis=2)
        zero = jnp.zeros((STEP, STEP, lanes), jnp.float32)
        shifted = [
            jnp.concatenate([zero] * b + [cot] + [zero] * (2 - b), axis=1).astype(jnp.bfloat16)
            for b in range(3)
        ]
        y = jnp.concatenate(shifted, axis=2).reshape(STEP * span, 3 * lanes)
        product_ref[...] += lax.dot_general(
            x, y, (((0,), (0,)), ((), ())), preferred_element_type=jnp.float32
        )
        back = lax.dot_general(
            y, weight_ref[...], (((1,), (1,)), ((), ())), preferred_element_type=jnp.float32
        ).reshape(STEP, span, 3 * lanes)
        for a in range(3):
            grad_ref[n + a] += back[:, :, a * lanes : (a + 1) * lanes]
        return carry

    lax.fori_loop(0, blocks, convolve, 0)

    def reduce(m, carry):
        u_total, v_total = carry
        at = pl.ds(pl.multiple_of(m * STEP, STEP), STEP)
        grad = grad_ref[m] * slope_ref[m]
        u_sum_ref[at] = jnp.sum(grad * u_col[None], axis=1)
        v_sum_ref[at] = jnp.sum(grad, axis=1)
        u_total = u_total + jnp.sum(grad * u_row_ref[at][:, None, :], axis=0)
        return u_total, v_total + jnp.sum(grad, axis=0)

    nothing = jnp.zeros((span, lanes), jnp.float32)
    u_total, v_total = lax.fori_loop(0, blocks + 2, reduce, (nothing, nothing))

    bins_ref[...] = jnp.zeros_like(bins_ref)
    u_sum, v_sum = u_sum_ref[...], v_sum_ref[...]
    at = pl.ds(pl.multiple_of(row0, STEP), depth)
    bins_ref[at] += jnp.where(in_first, u_sum, swap(v_sum))
    at = pl.ds(pl.multiple_of(row0 + half, STEP), depth)
    bins_ref[at] += jnp.where(in_first, swap(u_sum), v_sum)
    at = pl.ds(pl.multiple_of(col0, STEP), span)
    bins_ref[at] += jnp.where(in_first_col, u_total + swap(u_total), v_total + swap(v_total))

    for a in range(3):
        for b in range(3):
            block = product_ref[a * lanes : (a + 1) * lanes, b * lanes : (b + 1) * lanes]
            tap = (3 * a + b) * channels
            flat_ref[tap : tap + channels] = block[:channels, :channels] + block[channels:, channels:]
    taps = 9 * channels // 2
    packed_ref[...] = jnp.zeros_like(packed_ref)
    packed_ref[:taps] = jnp.concatenate([flat_ref[:taps], flat_ref[taps:]], axis=1)
    for r in range(n_row):
        part_ref[r, :chunk] = packed_ref[r * chunk : (r + 1) * chunk]
        part_ref[r, chunk:] = bins_ref[STEP + r * rows : STEP + (r + 1) * rows]

    for n in range(blocks):
        for h in range(2):
            pred_copy(n, h).wait()


def total_kernel(
    n_row,
    n_col,
    chunk,
    piece,
    part_ref,
    taps_ref,
    bins_ref,
    from_row,
    partial,
    from_col,
    total,
    every,
    send_a,
    recv_a,
    send_b,
    recv_b,
    send_c,
    recv_c,
    send_d,
    recv_d,
):
    row, col = lax.axis_index("row"), lax.axis_index("col")
    size = part_ref.shape[1]
    row_peers = [lax.rem(row + d, n_row) for d in range(1, n_row)]
    col_peers = [lax.rem(col + d, n_col) for d in range(1, n_col)]
    barrier = pltpu.get_barrier_semaphore()
    for peer in row_peers:
        signal(barrier, peer, col)
    for peer in col_peers:
        signal(barrier, row, peer)
    pl.semaphore_wait(barrier, n_row + n_col - 2)

    copies = []
    for d, peer in enumerate(row_peers):
        copy = remote(
            part_ref.at[peer], from_row.at[d], send_a.at[d], recv_a.at[d], peer, col
        )
        copy.start()
        copies.append(copy)
    if n_col * piece > size:
        partial[size:] = jnp.zeros((n_col * piece - size, partial.shape[1]), jnp.float32)
    for copy in copies:
        copy.wait()
    mine = part_ref[row]
    for d in range(n_row - 1):
        mine = mine + from_row[d]
    partial[:size] = mine

    def rows_of(owner):
        return pl.ds(pl.multiple_of(owner * piece, STEP), piece)

    copies = []
    for d, peer in enumerate(col_peers):
        copy = remote(
            partial.at[rows_of(peer)], from_col.at[d], send_b.at[d], recv_b.at[d], row, peer
        )
        copy.start()
        copies.append(copy)
    for copy in copies:
        copy.wait()
    mine = partial[rows_of(col)]
    for d in range(n_col - 1):
        mine = mine + from_col[d]
    total[rows_of(col)] = mine

    copies = []
    for d, peer in enumerate(col_peers):
        copy = remote(
            total.at[rows_of(col)], total.at[rows_of(col)], send_c.at[d], recv_c.at[d], row, peer
        )
        copy.start()
        copies.append(copy)
    for copy in copies:
        copy.wait()

    here = pl.ds(pl.multiple_of(row * chunk, STEP), chunk)
    every[here] = total[:chunk]
    copies = []
    for d, peer in enumerate(row_peers):
        copy = remote(
            total.at[pl.ds(0, chunk)], every.at[here], send_d.at[d], recv_d.at[d], peer, col
        )
        copy.start()
        copies.append(copy)
    bins_ref[...] = total[chunk:size]
    for copy in copies:
        copy.wait()
    taps, channels = taps_ref.shape
    taps_ref[: taps // 2] = every[: taps // 2, :channels]
    taps_ref[taps // 2 :] = every[: taps // 2, channels:]


def round_up(value, step):
    return -(-value // step) * step


def on_device(n_row, n_col, embedding, kernel, cotangent):
    rows, columns, channels = cotangent.shape
    lanes = 2 * channels
    bins = n_row * rows
    half = rows // 2
    blocks = half // STEP
    span = columns + 2 * STEP
    depth = half + 2 * STEP
    f32, bf16 = jnp.float32, jnp.bfloat16
    dma = pltpu.SemaphoreType.DMA
    wide = pl.pallas_call(
        functools.partial(gather_kernel, n_row),
        out_shape=jax.ShapeDtypeStruct((bins + 2 * STEP, lanes), f32),
        in_specs=[VMEM],
        out_specs=VMEM,
        scratch_shapes=[
            pltpu.VMEM((n_row - 1, rows, lanes), bf16),
            dma((n_row - 1,)),
            dma((n_row - 1,)),
        ],
        compiler_params=pltpu.CompilerParams(collective_id=0, has_side_effects=True),
        name="gather_embeddings",
    )(embedding)

    taps = 9 * channels
    chunk = round_up(-(-taps // (2 * n_row)), STEP)
    size = chunk + rows
    piece = round_up(-(-size // n_col), STEP)
    prediction, part = pl.pallas_call(
        functools.partial(tile_kernel, n_row, chunk),
        out_shape=(
            jax.ShapeDtypeStruct((rows, columns, channels), f32),
            jax.ShapeDtypeStruct((n_row, size, lanes), f32),
        ),
        in_specs=[VMEM, VMEM, ANY],
        out_specs=(ANY, VMEM),
        scratch_shapes=[
            pltpu.VMEM((rows, columns, channels), bf16),
            pltpu.VMEM((rows, columns, channels), f32),
            pltpu.VMEM((3 * lanes, 3 * lanes), bf16),
            pltpu.VMEM((depth, lanes), f32),
            pltpu.VMEM((depth, lanes), f32),
            pltpu.VMEM((blocks + 2, STEP * span, lanes), bf16),
            pltpu.VMEM((blocks + 2, STEP, span, lanes), f32),
            pltpu.VMEM((blocks + 2, STEP, span, lanes), f32),
            pltpu.VMEM((3 * lanes, 3 * lanes), f32),
            pltpu.VMEM((depth, lanes), f32),
            pltpu.VMEM((depth, lanes), f32),
            pltpu.VMEM((bins + 2 * STEP, lanes), f32),
            pltpu.VMEM((taps, channels), f32),
            pltpu.VMEM((n_row * chunk, lanes), f32),
            dma((blocks, 2)),
            dma((blocks, 2)),
        ],
        compiler_params=pltpu.CompilerParams(vmem_limit_bytes=48 * 2**20),
        name="tile_gradients",
    )(wide, kernel, cotangent)

    grad_kernel, grad_bins = pl.pallas_call(
        functools.partial(total_kernel, n_row, n_col, chunk, piece),
        out_shape=(
            jax.ShapeDtypeStruct((taps, channels), f32),
            jax.ShapeDtypeStruct((rows, lanes), f32),
        ),
        in_specs=[VMEM],
        out_specs=(VMEM, VMEM),
        scratch_shapes=[
            pltpu.VMEM((n_row - 1, size, lanes), f32),
            pltpu.VMEM((n_col * piece, lanes), f32),
            pltpu.VMEM((n_col - 1, piece, lanes), f32),
            pltpu.VMEM((n_col * piece, lanes), f32),
            pltpu.VMEM((n_row * chunk, lanes), f32),
        ]
        + [dma((n_row - 1,))] * 2
        + [dma((n_col - 1,))] * 4
        + [dma((n_row - 1,))] * 2,
        compiler_params=pltpu.CompilerParams(
            collective_id=1, has_side_effects=True, vmem_limit_bytes=32 * 2**20
        ),
        name="sum_gradients",
    )(part)
    return (
        prediction,
        grad_kernel.reshape(kernel.shape) / bins,
        grad_bins * float(bins) ** (-0.5),
    )


def solution(mesh):
    in_specs = (P("row", None), P(), P("row", "col", None))
    out_specs = (P("row", "col", None), P(), P("row", None))
    return jax.shard_map(
        functools.partial(on_device, mesh.shape["row"], mesh.shape["col"]),
        mesh=mesh,
        in_specs=in_specs,
        out_specs=out_specs,
        check_vma=False,
    )
```

time: 350 us -> 56.3 us (0.16)
  waiting for transfers between devices: 227 us -> 0 us
  Pallas kernels: 0 us -> 45.3 us
  matrix products: 41.3 us -> 0 us
  blocking collectives: 24.9 us -> 0 us
  starting transfers between devices: 19.9 us -> 0 us
  between operations: 14.2 us -> 0.69 us
  other arithmetic: 13 us -> 1.37 us
    psum x3 -> x0, waiting for transfers between devices: 216 us -> none  [the longest x1 73 us: from_root(): return lax.psum(jnp.where(mine, shard, jnp.zeros_like(shard)), axis)]
    pallas_call x0 -> x3, Pallas kernels: none -> 45.3 us  [the longest x1 23.6 us: on_device(): pl.pallas_call(functools.partial(total_kernel, n_row, n_col, chunk, piece...]
    dot_general x27 -> x0, matrix products: 41.3 us -> none  [the longest x9 23.3 us: on_device(): jnp.einsum('ijc,cd->ijd', shifted_pairs, kernel[kernel_tap_row, kernel_ta...]
    psum x2 -> x0, blocking collectives: 24.9 us -> none  [the longest x1 12.7 us: from_root(): return lax.psum(jnp.where(mine, shard, jnp.zeros_like(shard)), axis)]
    ppermute x8 -> x0, starting transfers between devices: 19.6 us -> none  [the longest x4 14.3 us: padded(): lax.ppermute(tail, axis, [(i, (i + 1) % count) for i in range(ends)])]
    ppermute x8 -> x0, waiting for transfers between devices: 10.6 us -> none  [the longest x4 6.97 us: padded(): lax.ppermute(tail, axis, [(i, (i + 1) % count) for i in range(ends)])]
    unnamed x18 -> x6, local copies, waits for them, and re-layouts: 2.91 us -> 8.76 us
    add x1 -> x0, other arithmetic: 4.19 us -> none  [build_pairs(): row_embedding[:, None, :channels] * col_embed[None, :, :channels]]
  transfers between devices with their start and end apart: 11 -> 0, of which waited for: 5 -> 0; matrix products, arithmetic and copies ran while one was open for 17% -> 0% of each run, Pallas kernels for 0% -> 0%
where the time goes in v1:
time: 56.3 us; the launch traced here: 56.2 us
  Pallas kernels  45.3 us (80%)
  local copies, waits for them, and re-layouts  8.76 us (16%)
  other arithmetic  1.37 us (2%)
  between operations  0.69 us (1%)
    pallas_call x1, Pallas kernels, on_device(): pl.pallas_call(functools.partial(total_kernel, n_row, n_col, chunk, piece...  23.6 us
    pallas_call x1, Pallas kernels, on_device(): pl.pallas_call(functools.partial(tile_kernel, n_row, chunk), out_shape=(j...  15 us
    unnamed x6, local copies, waits for them, and re-layouts  8.76 us
    pallas_call x1, Pallas kernels, on_device(): pl.pallas_call(functools.partial(gather_kernel, n_row), out_shape=jax.Sha...  6.78 us

profile of v1, /device:TPU:0, one launch (start us, length us, event | category | flops | bytes accessed | tf_op | source)
XLA Modules:
  0.0 56.2 jit_solution(4661890118604575236)
XLA Ops:
  0.6 0.0 copy-start.1
  0.6 6.8 %gather_embeddings.1.wide_ref = f32[528,128]{1,0:T(8,128)} custom-call(bf16[128,128]{1,0:T(8,128)(2,1)} %emb_ref.1), custom_call_target="tpu_custom_call" | custom-call | tf_op jit(solution)/shard_map/gather_embeddings/pallas_call | solution.py:330
  7.4 0.0 copy-start
  7.4 4.0 %copy.6.cot_hbm = bf16[128,64,64]{2,1,0:T(8,128)(2,1)S(1)} copy(bf16[128,64,64]{0,2,1:T(8,128)(2,1)} %param.5) | data formatting | bytes 2097152 | tf_op args[2]
  11.4 0.0 copy-done.1
  11.4 0.0 copy-done
  11.4 15.0 %tile_gradients.1 = (f32[128,64,64]{2,1,0:T(8,128)}, f32[4,200,128]{2,1,0:T(8,128)S(1)}) custom-call(f32[528,128]{1,0:T(8,128)S(1)} %copy-done, bf16[3,3,64,64]{3,2,1,0:T(8,128)(2,1)S(1)} %copy-done.1, bf16[128,64,64]{2,1,0:T(8,128)(2,1)S(1)} %copy.6.cot_hbm), custom_call_target="tpu_custom_call" | custom-call | tf_op jit(solution)/shard_map/tile_gradients/pallas_call | solution.py:348
  26.4 4.8 %copy.7 = f32[128,64,64]{0,2,1:T(8,128)} copy(f32[128,64,64]{2,1,0:T(8,128)} %get-tuple-element.11) | data formatting | bytes 4194304
  31.2 23.6 %sum_gradients.1 = (f32[576,64]{1,0:T(8,128)S(1)}, f32[128,128]{1,0:T(8,128)S(1)}) custom-call(f32[4,200,128]{2,1,0:T(8,128)S(1)} %get-tuple-element.8.part_ref), custom_call_target="tpu_custom_call" | custom-call | tf_op jit(solution)/shard_map/sum_gradients/pallas_call | solution.py:378
  54.8 0.7 %broadcast_multiply_fusion = f32[576,64]{1,0:T(8,128)} fusion(f32[576,64]{1,0:T(8,128)S(1)} %get-tuple-element.9), kind=kLoop, calls=%fused_computation | loop fusion | flops 36864 | bytes 294912 | tf_op jit(solution)/shard_map/div | solution.py:403
  55.5 0.6 %broadcast_multiply_fusion.1 = f32[128,128]{1,0:T(8,128)} fusion(f32[128,128]{1,0:T(8,128)S(1)} %get-tuple-element.10), kind=kLoop, calls=%fused_computation.1 | loop fusion | flops 16384 | bytes 131072 | tf_op jit(solution)/shard_map/mul | solution.py:404
Async XLA Ops:
  0.6 10.8 %copy-start.1 = (bf16[3,3,64,64]{3,2,1,0:T(8,128)(2,1)S(1)}, bf16[3,3,64,64]{3,2,1,0:T(8,128)(2,1)}, u32[]{:S(2)}) copy-start(bf16[3,3,64,64]{3,2,1,0:T(8,128)(2,1)} %kernel_ref.1) | copy-start | bytes 221188
  7.4 4.0 %copy-start = (f32[528,128]{1,0:T(8,128)S(1)}, f32[528,128]{1,0:T(8,128)}, u32[]{:S(2)}) copy-start(f32[528,128]{1,0:T(8,128)} %gather_embeddings.1.wide_ref) | copy-start | bytes 811012

commit v2 on v1

v2 whole, which is shorter than its diff:
```python
import functools

import jax
import jax.numpy as jnp
from jax import lax
from jax.experimental import pallas as pl
from jax.experimental.pallas import tpu as pltpu
from jax.sharding import PartitionSpec as P

STEP = 8
MESH = pl.DeviceIdType.MESH
VMEM = pl.BlockSpec(memory_space=pltpu.VMEM)
ANY = pl.BlockSpec(memory_space=pl.ANY)


def signal(barrier, row, col):
    pl.semaphore_signal(barrier, inc=1, device_id=(row, col), device_id_type=MESH)


def remote(src, dst, send, recv, row, col):
    return pltpu.make_async_remote_copy(
        src_ref=src,
        dst_ref=dst,
        send_sem=send,
        recv_sem=recv,
        device_id=(row, col),
        device_id_type=MESH,
    )


def gather_kernel(n_row, emb_ref, out_ref, held, send_sem, recv_sem):
    row, col = lax.axis_index("row"), lax.axis_index("col")
    rows = emb_ref.shape[0]
    barrier = pltpu.get_barrier_semaphore()
    peers = [lax.rem(row + d, n_row) for d in range(1, n_row)]
    for peer in peers:
        signal(barrier, peer, col)
    pl.semaphore_wait(barrier, n_row - 1)
    copies = []
    for d, peer in enumerate(peers):
        copy = remote(emb_ref, held.at[d], send_sem.at[d], recv_sem.at[d], peer, col)
        copy.start()
        copies.append(copy)
    border = jnp.zeros((STEP, out_ref.shape[1]), jnp.float32)
    out_ref[:STEP] = border
    out_ref[STEP + n_row * rows :] = border
    out_ref[pl.ds(pl.multiple_of(STEP + row * rows, STEP), rows)] = emb_ref[...].astype(jnp.float32)
    for d, copy in enumerate(copies):
        copy.wait()
        owner = lax.rem(row + n_row - 1 - d, n_row)
        out_ref[pl.ds(pl.multiple_of(STEP + owner * rows, STEP), rows)] = held[d].astype(
            jnp.float32
        )


def tile_kernel(
    wide_ref,
    kernel_ref,
    cot_hbm,
    pred_hbm,
    packed_ref,
    row_ref,
    col_ref,
    cot_ref,
    pred_ref,
    weight_ref,
    u_col_ref,
    v_col_ref,
    act_ref,
    slope_ref,
    grad_ref,
    product_ref,
    u_sum_ref,
    v_sum_ref,
    flat_ref,
    cot_sem,
    pred_sem,
):
    columns, channels, rows = cot_ref.shape
    half = columns // 2
    blocks = half // STEP
    span = rows + 2 * STEP
    lanes = 2 * channels
    bins = wide_ref.shape[0] - 2 * STEP
    row0 = lax.axis_index("row") * rows
    col0 = lax.axis_index("col") * columns

    def cot_copy(n, h):
        at = pl.ds(h * half + n * STEP, STEP)
        return pltpu.make_async_copy(cot_hbm.at[at], cot_ref.at[at], cot_sem.at[n, h])

    def pred_copy(n, h):
        at = pl.ds(h * half + n * STEP, STEP)
        return pltpu.make_async_copy(pred_ref.at[at], pred_hbm.at[at], pred_sem.at[n, h])

    for n in range(blocks):
        for h in range(2):
            cot_copy(n, h).start()

    none = jnp.zeros((channels, channels), jnp.float32)
    for a in range(3):
        for b in range(3):
            w = kernel_ref[a, b].astype(jnp.float32)
            both = jnp.concatenate(
                [jnp.concatenate([w, none], axis=1), jnp.concatenate([none, w], axis=1)], axis=0
            )
            weight_ref[b * lanes : (b + 1) * lanes, a * lanes : (a + 1) * lanes] = both.astype(
                jnp.bfloat16
            )

    def first(shape):
        return lax.broadcasted_iota(jnp.int32, shape, len(shape) - 1) < channels

    def swap(x):
        return pltpu.roll(x, channels, 1)

    depth = half + 2 * STEP
    low = wide_ref[pl.ds(pl.multiple_of(col0, STEP), depth)]
    high = wide_ref[pl.ds(pl.multiple_of(col0 + half, STEP), depth)]
    in_first = first((depth, lanes))
    u_col_ref[...] = jnp.where(in_first, low, swap(high))
    v_col_ref[...] = jnp.where(in_first, swap(low), high)
    side = wide_ref[pl.ds(pl.multiple_of(row0, STEP), span)]
    in_first_row = first((span, lanes))
    u_row = jnp.where(in_first_row, side, swap(side))
    v_row = jnp.where(in_first_row, swap(side), side)
    row_pos = row0 - STEP + lax.broadcasted_iota(jnp.int32, (span, lanes), 0)
    row_in = jnp.where((row_pos >= 0) & (row_pos < bins), 1.0, 0.0)

    def activate(m, carry):
        at = pl.ds(pl.multiple_of(m * STEP, STEP), STEP)
        shape = (STEP, 1, lanes)
        pos = col0 - STEP + m * STEP + lax.broadcasted_iota(jnp.int32, shape, 0)
        pos = pos + jnp.where(first(shape), 0, half)
        col_in = jnp.where((pos >= 0) & (pos < bins), 1.0, 0.0)
        pairs = u_col_ref[at][:, None, :] * u_row[None] + v_col_ref[at][:, None, :] + v_row[None]
        s = 0.5 * jnp.tanh(0.5 * pairs) + 0.5
        s = s * (col_in * row_in[None])
        act = pairs * s
        act_ref[m] = act.reshape(STEP * span, lanes).astype(jnp.bfloat16)
        slope_ref[m] = s + act * (1.0 - s)
        grad_ref[m] = jnp.zeros((STEP, span, lanes), jnp.float32)
        return carry

    lax.fori_loop(0, blocks + 2, activate, 0)
    product_ref[...] = jnp.zeros_like(product_ref)

    def convolve(n, carry):
        for h in range(2):
            cot_copy(n, h).wait()
        x = jnp.concatenate([act_ref[n + b] for b in range(3)], axis=1)
        out = jnp.dot(x, weight_ref[...], preferred_element_type=jnp.float32)
        out = out.reshape(STEP, span, 3 * lanes)
        out = (
            out[:, :rows, :lanes]
            + out[:, STEP : STEP + rows, lanes : 2 * lanes]
            + out[:, 2 * STEP :, 2 * lanes :]
        )
        cot = []
        for k in range(STEP):
            at = n * STEP + k
            turned = out[k].T
            pred_ref[at] = turned[:channels]
            pred_ref[half + at] = turned[channels:]
            stack = jnp.concatenate([cot_ref[at], cot_ref[half + at]], axis=0)
            cot.append(stack.astype(jnp.float32).T)
        for h in range(2):
            pred_copy(n, h).start()
        cot = jnp.stack(cot)
        zero = jnp.zeros((STEP, STEP, lanes), jnp.float32)
        shifted = [
            jnp.concatenate([zero] * a + [cot] + [zero] * (2 - a), axis=1).astype(jnp.bfloat16)
            for a in range(3)
        ]
        y = jnp.concatenate(shifted, axis=2).reshape(STEP * span, 3 * lanes)
        product_ref[...] += lax.dot_general(
            x, y, (((0,), (0,)), ((), ())), preferred_element_type=jnp.float32
        )
        back = lax.dot_general(
            y, weight_ref[...], (((1,), (1,)), ((), ())), preferred_element_type=jnp.float32
        ).reshape(STEP, span, 3 * lanes)
        for b in range(3):
            grad_ref[n + b] += back[:, :, b * lanes : (b + 1) * lanes]
        return carry

    lax.fori_loop(0, blocks, convolve, 0)

    def reduce(m, carry):
        u_total, v_total = carry
        at = pl.ds(pl.multiple_of(m * STEP, STEP), STEP)
        grad = grad_ref[m] * slope_ref[m]
        u_sum_ref[at] = jnp.sum(grad * u_row[None], axis=1)
        v_sum_ref[at] = jnp.sum(grad, axis=1)
        u_total = u_total + jnp.sum(grad * u_col_ref[at][:, None, :], axis=0)
        return u_total, v_total + jnp.sum(grad, axis=0)

    nothing = jnp.zeros((span, lanes), jnp.float32)
    u_total, v_total = lax.fori_loop(0, blocks + 2, reduce, (nothing, nothing))

    row_ref[...] = jnp.where(in_first_row, u_total + swap(u_total), v_total + swap(v_total))
    u_sum, v_sum = u_sum_ref[...], v_sum_ref[...]
    col_ref[:depth] = jnp.where(in_first, u_sum, swap(v_sum))
    col_ref[depth:] = jnp.zeros((half, lanes), jnp.float32)
    col_ref[half:] += jnp.where(in_first, swap(u_sum), v_sum)

    for a in range(3):
        for b in range(3):
            block = product_ref[b * lanes : (b + 1) * lanes, a * lanes : (a + 1) * lanes]
            tap = (3 * a + b) * channels
            flat_ref[tap : tap + channels] = block[:channels, :channels] + block[channels:, channels:]
    taps = 9 * channels // 2
    packed_ref[:taps] = jnp.concatenate([flat_ref[:taps], flat_ref[taps:]], axis=1)
    if packed_ref.shape[0] > taps:
        packed_ref[taps:] = jnp.zeros((packed_ref.shape[0] - taps, lanes), jnp.float32)

    for n in range(blocks):
        for h in range(2):
            pred_copy(n, h).wait()


def total_kernel(
    n_row,
    n_col,
    chunk,
    piece,
    columns,
    packed_ref,
    row_ref,
    col_ref,
    taps_ref,
    bins_ref,
    from_row,
    from_owned,
    partial,
    from_col,
    total,
    every,
    border,
    send_a,
    recv_a,
    send_b,
    recv_b,
    send_c,
    recv_c,
    send_d,
    recv_d,
    send_e,
    recv_e,
    send_f,
    recv_f,
):
    row, col = lax.axis_index("row"), lax.axis_index("col")
    span = row_ref.shape[0]
    rows = span - 2 * STEP
    size = chunk + span
    ratio = rows // columns
    owner = col // ratio
    row_peers = [lax.rem(row + d, n_row) for d in range(1, n_row)]
    col_peers = [lax.rem(col + d, n_col) for d in range(1, n_col)]
    barrier = pltpu.get_barrier_semaphore()
    for peer in row_peers:
        signal(barrier, peer, col)
    for peer in col_peers:
        signal(barrier, row, peer)
    pl.semaphore_wait(barrier, n_row + n_col - 2)

    def rows_at(index, count):
        return pl.ds(pl.multiple_of(index * count, STEP), count)

    away = lax.rem(owner + n_row - row, n_row) - 1

    def owned_copy(d, target):
        return remote(col_ref, from_owned.at[d], send_e.at[0], recv_e.at[d], target, col)

    @pl.when(row != owner)
    def _():
        owned_copy(away, owner).start()

    copies = []
    for d, peer in enumerate(row_peers):
        copy = remote(
            packed_ref.at[rows_at(peer, chunk)],
            from_row.at[d],
            send_a.at[d],
            recv_a.at[d],
            peer,
            col,
        )
        copy.start()
        copies.append(copy)
    if n_col * piece > size:
        partial[size:] = jnp.zeros((n_col * piece - size, partial.shape[1]), jnp.float32)
    partial[chunk:size] = row_ref[...]

    @pl.when(row == owner)
    def _():
        mine = col_ref[...]
        for d in range(n_row - 1):
            owned_copy(d, row_peers[0]).wait_recv()
            mine = mine + from_owned[d]
        start = chunk + lax.rem(col, ratio) * columns
        partial[pl.ds(pl.multiple_of(start, STEP), columns + 2 * STEP)] += mine

    @pl.when(row != owner)
    def _():
        owned_copy(away, owner).wait_send()

    for copy in copies:
        copy.wait()
    mine = packed_ref[rows_at(row, chunk)]
    for d in range(n_row - 1):
        mine = mine + from_row[d]
    partial[:chunk] = mine

    copies = []
    for d, peer in enumerate(col_peers):
        copy = remote(
            partial.at[rows_at(peer, piece)], from_col.at[d], send_b.at[d], recv_b.at[d], row, peer
        )
        copy.start()
        copies.append(copy)
    for copy in copies:
        copy.wait()
    mine = partial[rows_at(col, piece)]
    for d in range(n_col - 1):
        mine = mine + from_col[d]
    here = rows_at(col, piece)
    total[here] = mine

    copies = []
    for d, peer in enumerate(col_peers):
        copy = remote(total.at[here], total.at[here], send_c.at[d], recv_c.at[d], row, peer)
        copy.start()
        copies.append(copy)
    for copy in copies:
        copy.wait()

    below, above = lax.rem(row + n_row - 1, n_row), lax.rem(row + 1, n_row)
    copies = []
    for d, (peer, start) in enumerate([(below, chunk), (above, size - STEP)]):
        copy = remote(
            total.at[pl.ds(start, STEP)], border.at[d], send_f.at[d], recv_f.at[d], peer, col
        )
        copy.start()
        copies.append(copy)
    here = rows_at(row, chunk)
    for d, peer in enumerate(row_peers):
        copy = remote(
            total.at[pl.ds(0, chunk)], every.at[here], send_d.at[d], recv_d.at[d], peer, col
        )
        copy.start()
        copies.append(copy)
    every[here] = total[:chunk]
    bins_ref[...] = total[chunk + STEP : size - STEP]
    for copy in copies:
        copy.wait()
    bins_ref[rows - STEP :] += border[0]
    bins_ref[:STEP] += border[1]
    taps, channels = taps_ref.shape
    taps_ref[: taps // 2] = every[: taps // 2, :channels]
    taps_ref[taps // 2 :] = every[: taps // 2, channels:]


def round_up(value, step):
    return -(-value // step) * step


def on_device(n_row, n_col, embedding, kernel, cotangent):
    rows, columns, channels = cotangent.shape
    lanes = 2 * channels
    bins = n_row * rows
    half = columns // 2
    blocks = half // STEP
    span = rows + 2 * STEP
    depth = half + 2 * STEP
    f32, bf16 = jnp.float32, jnp.bfloat16
    dma = pltpu.SemaphoreType.DMA
    wide = pl.pallas_call(
        functools.partial(gather_kernel, n_row),
        out_shape=jax.ShapeDtypeStruct((bins + 2 * STEP, lanes), f32),
        in_specs=[VMEM],
        out_specs=VMEM,
        scratch_shapes=[
            pltpu.VMEM((n_row - 1, rows, lanes), bf16),
            dma((n_row - 1,)),
            dma((n_row - 1,)),
        ],
        compiler_params=pltpu.CompilerParams(collective_id=0, has_side_effects=True),
        name="gather_embeddings",
    )(embedding)

    taps = 9 * channels
    chunk = round_up(-(-taps // (2 * n_row)), STEP)
    size = chunk + span
    piece = round_up(-(-size // n_col), STEP)
    prediction, packed, row_part, col_part = pl.pallas_call(
        tile_kernel,
        out_shape=(
            jax.ShapeDtypeStruct((columns, channels, rows), f32),
            jax.ShapeDtypeStruct((n_row * chunk, lanes), f32),
            jax.ShapeDtypeStruct((span, lanes), f32),
            jax.ShapeDtypeStruct((columns + 2 * STEP, lanes), f32),
        ),
        in_specs=[VMEM, VMEM, ANY],
        out_specs=(ANY, VMEM, VMEM, VMEM),
        scratch_shapes=[
            pltpu.VMEM((columns, channels, rows), bf16),
            pltpu.VMEM((columns, channels, rows), f32),
            pltpu.VMEM((3 * lanes, 3 * lanes), bf16),
            pltpu.VMEM((depth, lanes), f32),
            pltpu.VMEM((depth, lanes), f32),
            pltpu.VMEM((blocks + 2, STEP * span, lanes), bf16),
            pltpu.VMEM((blocks + 2, STEP, span, lanes), f32),
            pltpu.VMEM((blocks + 2, STEP, span, lanes), f32),
            pltpu.VMEM((3 * lanes, 3 * lanes), f32),
            pltpu.VMEM((depth, lanes), f32),
            pltpu.VMEM((depth, lanes), f32),
            pltpu.VMEM((taps, channels), f32),
            dma((blocks, 2)),
            dma((blocks, 2)),
        ],
        compiler_params=pltpu.CompilerParams(vmem_limit_bytes=48 * 2**20),
        name="tile_gradients",
    )(wide, kernel, cotangent.transpose(1, 2, 0))

    grad_kernel, grad_bins = pl.pallas_call(
        functools.partial(total_kernel, n_row, n_col, chunk, piece, columns),
        out_shape=(
            jax.ShapeDtypeStruct((taps, channels), f32),
            jax.ShapeDtypeStruct((rows, lanes), f32),
        ),
        in_specs=[VMEM, VMEM, VMEM],
        out_specs=(VMEM, VMEM),
        scratch_shapes=[
            pltpu.VMEM((n_row - 1, chunk, lanes), f32),
            pltpu.VMEM((n_row - 1, columns + 2 * STEP, lanes), f32),
            pltpu.VMEM((n_col * piece, lanes), f32),
            pltpu.VMEM((n_col - 1, piece, lanes), f32),
            pltpu.VMEM((n_col * piece, lanes), f32),
            pltpu.VMEM((n_row * chunk, lanes), f32),
            pltpu.VMEM((2, STEP, lanes), f32),
        ]
        + [dma((n_row - 1,))] * 2
        + [dma((n_col - 1,))] * 4
        + [dma((n_row - 1,))] * 2
        + [dma((1,)), dma((n_row - 1,)), dma((2,)), dma((2,))],
        compiler_params=pltpu.CompilerParams(
            collective_id=1, has_side_effects=True, vmem_limit_bytes=32 * 2**20
        ),
        name="sum_gradients",
    )(packed, row_part, col_part)
    return (
        prediction.transpose(2, 0, 1),
        grad_kernel.reshape(kernel.shape) / bins,
        grad_bins * float(bins) ** (-0.5),
    )


def solution(mesh):
    in_specs = (P("row", None), P(), P("row", "col", None))
    out_specs = (P("row", "col", None), P(), P("row", None))
    return jax.shard_map(
        functools.partial(on_device, mesh.shape["row"], mesh.shape["col"]),
        mesh=mesh,
        in_specs=in_specs,
        out_specs=out_specs,
        check_vma=False,
    )
```

time: 56.3 us -> 45.9 us (0.82)
  local copies, waits for them, and re-layouts: 8.76 us -> 3.08 us
  Pallas kernels: 45.3 us -> 40.5 us
    unnamed x6, local copies, waits for them, and re-layouts: 8.76 us -> 3.08 us
    pallas_call x1, Pallas kernels: 15 us -> 12.2 us  [on_device(): pl.pallas_call(tile_kernel, out_shape=(jax.ShapeDtypeStruct((columns, cha...]
    pallas_call x1, Pallas kernels: 23.6 us -> 21.6 us  [on_device(): pl.pallas_call(functools.partial(total_kernel, n_row, n_col, chunk, piece...]
where the time goes in v2:
time: 45.9 us; the launch traced here: 45.6 us
  Pallas kernels  40.5 us (88%)
  local copies, waits for them, and re-layouts  3.08 us (7%)
  other arithmetic  1.37 us (3%)
  between operations  0.66 us (1%)
    pallas_call x1, Pallas kernels, on_device(): pl.pallas_call(functools.partial(total_kernel, n_row, n_col, chunk, piece...  21.6 us
    pallas_call x1, Pallas kernels, on_device(): pl.pallas_call(tile_kernel, out_shape=(jax.ShapeDtypeStruct((columns, cha...  12.2 us
    pallas_call x1, Pallas kernels, on_device(): pl.pallas_call(functools.partial(gather_kernel, n_row), out_shape=jax.Sha...  6.76 us
    unnamed x6, local copies, waits for them, and re-layouts  3.08 us

profile of v2, /device:TPU:0, one launch (start us, length us, event | category | flops | bytes accessed | tf_op | source)
XLA Modules:
  0.0 45.6 jit_solution(8448611921196034228)
XLA Ops:
  0.6 6.8 %gather_embeddings.1.wide_ref = f32[528,128]{1,0:T(8,128)} custom-call(bf16[128,128]{1,0:T(8,128)(2,1)} %emb_ref.1), custom_call_target="tpu_custom_call" | custom-call | tf_op jit(solution)/shard_map/gather_embeddings/pallas_call | solution.py:378
  7.4 0.0 copy-start
  7.4 0.9 %copy-done = f32[528,128]{1,0:T(8,128)S(1)} copy-done((f32[528,128]{1,0:T(8,128)S(1)}, f32[528,128]{1,0:T(8,128)}, u32[]{:S(2)}) %copy-start) | copy-done | bytes 270360
  8.3 0.0 copy-start.1
  8.3 1.2 %copy-done.1 = bf16[128,64,64]{0,2,1:T(8,128)(2,1)S(1)} copy-done((bf16[128,64,64]{0,2,1:T(8,128)(2,1)S(1)}, bf16[128,64,64]{0,2,1:T(8,128)(2,1)}, u32[]{:S(2)}) %copy-start.1) | copy-done | bytes 1048600
  9.6 0.0 copy-start.2
  9.6 0.9 %copy-done.2 = bf16[3,3,64,64]{3,2,1,0:T(8,128)(2,1)S(1)} copy-done((bf16[3,3,64,64]{3,2,1,0:T(8,128)(2,1)S(1)}, bf16[3,3,64,64]{3,2,1,0:T(8,128)(2,1)}, u32[]{:S(2)}) %copy-start.2) | copy-done | bytes 73752
  10.5 12.2 %tile_gradients.1 = (f32[64,64,128]{2,1,0:T(8,128)}, f32[288,128]{1,0:T(8,128)S(1)}, f32[144,128]{1,0:T(8,128)S(1)}, f32[80,128]{1,0:T(8,128)S(1)}) custom-call(f32[528,128]{1,0:T(8,128)S(1)} %copy-done, bf16[3,3,64,64]{3,2,1,0:T(8,128)(2,1)S(1)} %copy-done.2, bf16[64,64,128]{2,1,0:T(8,128)(2,1)S(1)} %bitcast.3), custom_call_target="tpu_custom_call" | custom-call | tf_op jit(solution)/shard_map/tile_gradients/pallas_call | solution.py:396
  22.7 21.6 %sum_gradients.1 = (f32[576,64]{1,0:T(8,128)S(1)}, f32[128,128]{1,0:T(8,128)S(1)}) custom-call(f32[288,128]{1,0:T(8,128)S(1)} %get-tuple-element.10.packed_ref, f32[144,128]{1,0:T(8,128)S(1)} %get-tuple-element.11.row_ref, f32[80,128]{1,0:T(8,128)S(1)} %get-tuple-element.12.col_ref), custom_call_target="tpu_custom_call" | custom-call | tf_op jit(solution)/shard_map/sum_gradients/pallas_call | solution.py:426
  44.3 0.7 %broadcast_multiply_fusion = f32[576,64]{1,0:T(8,128)} fusion(f32[576,64]{1,0:T(8,128)S(1)} %get-tuple-element.13), kind=kLoop, calls=%fused_computation | loop fusion | flops 36864 | bytes 294912 | tf_op jit(solution)/shard_map/div | solution.py:454
  45.0 0.6 %broadcast_multiply_fusion.1 = f32[128,128]{1,0:T(8,128)} fusion(f32[128,128]{1,0:T(8,128)S(1)} %get-tuple-element.14), kind=kLoop, calls=%fused_computation.1 | loop fusion | flops 16384 | bytes 131072 | tf_op jit(solution)/shard_map/mul | solution.py:455
Async XLA Ops:
  7.4 1.0 %copy-start = (f32[528,128]{1,0:T(8,128)S(1)}, f32[528,128]{1,0:T(8,128)}, u32[]{:S(2)}) copy-start(f32[528,128]{1,0:T(8,128)} %gather_embeddings.1.wide_ref) | copy-start | bytes 811012
  8.3 1.2 %copy-start.1 = (bf16[128,64,64]{0,2,1:T(8,128)(2,1)S(1)}, bf16[128,64,64]{0,2,1:T(8,128)(2,1)}, u32[]{:S(2)}) copy-start(bf16[128,64,64]{0,2,1:T(8,128)(2,1)} %param.5) | copy-start | bytes 3145732
  9.6 0.9 %copy-start.2 = (bf16[3,3,64,64]{3,2,1,0:T(8,128)(2,1)S(1)}, bf16[3,3,64,64]{3,2,1,0:T(8,128)(2,1)}, u32[]{:S(2)}) copy-start(bf16[3,3,64,64]{3,2,1,0:T(8,128)(2,1)} %kernel_ref.1) | copy-start | bytes 221188

commit v3 on v0

v3 whole, which is shorter than its diff:
```python
import functools
import types

import jax
import jax.numpy as jnp
from jax import lax
from jax.experimental import pallas as pl
from jax.experimental.pallas import tpu as pltpu
from jax.sharding import PartitionSpec as P

STEP = 8
MESH = pl.DeviceIdType.MESH
VMEM = pl.BlockSpec(memory_space=pltpu.VMEM)
ANY = pl.BlockSpec(memory_space=pl.ANY)


def signal(barrier, row, col):
    pl.semaphore_signal(barrier, inc=1, device_id=(row, col), device_id_type=MESH)


def remote(src, dst, send, recv, row, col):
    return pltpu.make_async_remote_copy(
        src_ref=src,
        dst_ref=dst,
        send_sem=send,
        recv_sem=recv,
        device_id=(row, col),
        device_id_type=MESH,
    )


def tile_kernel(n_row, n_col, chunk, piece, refs):
    emb_hbm, kernel_hbm, cot_hbm = refs.emb_hbm, refs.kernel_hbm, refs.cot_hbm
    wide_ref, weight_ref, cot_ref, pred_ref = refs.wide, refs.weight, refs.cot, refs.pred
    act_ref, turned_ref, grad_ref, product_ref = refs.act, refs.turned, refs.grad, refs.product
    col_ref, partial, total, every = refs.col, refs.partial, refs.total, refs.every
    columns, channels, rows = cot_ref.shape
    half = columns // 2
    blocks = half // STEP
    span = rows + 2 * STEP
    depth = half + 2 * STEP
    lanes = 2 * channels
    bins = n_row * rows
    size = chunk + span
    ratio = rows // columns
    row, col = lax.axis_index("row"), lax.axis_index("col")
    row0, col0 = row * rows, col * columns
    owner = col // ratio
    row_peers = [lax.rem(row + d, n_row) for d in range(1, n_row)]
    col_peers = [lax.rem(col + d, n_col) for d in range(1, n_col)]

    def local(source, target, sem):
        return pltpu.make_async_copy(source, target, sem)

    def cot_copy(n, h):
        at = pl.ds(h * half + n * STEP, STEP)
        return local(cot_hbm.at[at], cot_ref.at[at], refs.cot_sem.at[n, h])

    def pred_copy(n, h):
        at = pl.ds(h * half + n * STEP, STEP)
        return local(pred_ref.at[at], refs.pred_hbm.at[at], refs.pred_sem.at[n, h])

    def rows_at(index, count):
        return pl.ds(pl.multiple_of(index * count, STEP), count)

    def start(copies):
        for copy in copies:
            copy.start()

    def wait(copies):
        for copy in copies:
            copy.wait()

    barrier = pltpu.get_barrier_semaphore()
    for peer in row_peers:
        signal(barrier, peer, col)
    for peer in col_peers:
        signal(barrier, row, peer)
    inputs = [
        local(emb_hbm, refs.emb, refs.in_sem.at[0]),
        local(kernel_hbm, refs.kernel, refs.in_sem.at[1]),
    ]
    start(inputs)
    start([cot_copy(n, h) for n in range(blocks) for h in range(2)])

    grad_ref[...] = jnp.zeros_like(grad_ref)
    product_ref[...] = jnp.zeros_like(product_ref)
    zeros = jnp.zeros((STEP, lanes), jnp.float32)
    wide_ref[:STEP] = zeros
    wide_ref[STEP + bins :] = zeros
    if n_col * piece > size:
        partial[size:] = jnp.zeros((n_col * piece - size, lanes), jnp.float32)

    wait(inputs)
    pl.semaphore_wait(barrier, n_row + n_col - 2)
    gather = [
        remote(refs.emb, refs.held.at[d], refs.send_g.at[d], refs.recv_g.at[d], peer, col)
        for d, peer in enumerate(row_peers)
    ]
    start(gather)

    none = jnp.zeros((channels, channels), jnp.float32)
    for a in range(3):
        for b in range(3):
            w = refs.kernel[a, b].astype(jnp.float32)
            both = jnp.concatenate(
                [jnp.concatenate([w, none], axis=1), jnp.concatenate([none, w], axis=1)], axis=0
            )
            weight_ref[b * lanes : (b + 1) * lanes, a * lanes : (a + 1) * lanes] = both.astype(
                jnp.bfloat16
            )

    def spread(n, carry):
        wait([cot_copy(n, h) for h in range(2)])
        cot = []
        for k in range(STEP):
            at = n * STEP + k
            stack = jnp.concatenate([cot_ref[at], cot_ref[half + at]], axis=0)
            cot.append(stack.astype(jnp.float32).T)
        cot = jnp.stack(cot)
        zero = jnp.zeros((STEP, STEP, lanes), jnp.float32)
        shifted = [
            jnp.concatenate([zero] * a + [cot] + [zero] * (2 - a), axis=1).astype(jnp.bfloat16)
            for a in range(3)
        ]
        y = jnp.concatenate(shifted, axis=2).reshape(STEP * span, 3 * lanes)
        turned_ref[n] = y
        back = lax.dot_general(
            y, weight_ref[...], (((1,), (1,)), ((), ())), preferred_element_type=jnp.float32
        ).reshape(STEP, span, 3 * lanes)
        for b in range(3):
            grad_ref[n + b] += back[:, :, b * lanes : (b + 1) * lanes]
        return carry

    lax.fori_loop(0, blocks, spread, 0)

    wide_ref[pl.ds(pl.multiple_of(STEP + row0, STEP), rows)] = refs.emb[...].astype(jnp.float32)
    for d, copy in enumerate(gather):
        copy.wait()
        peer = lax.rem(row + n_row - 1 - d, n_row)
        at = pl.ds(pl.multiple_of(STEP + peer * rows, STEP), rows)
        wide_ref[at] = refs.held[d].astype(jnp.float32)

    def first(shape):
        return lax.broadcasted_iota(jnp.int32, shape, len(shape) - 1) < channels

    def swap(x):
        return pltpu.roll(x, channels, 1)

    low = wide_ref[pl.ds(pl.multiple_of(col0, STEP), depth)]
    high = wide_ref[pl.ds(pl.multiple_of(col0 + half, STEP), depth)]
    in_first = first((depth, lanes))
    refs.u_col[...] = jnp.where(in_first, low, swap(high))
    refs.v_col[...] = jnp.where(in_first, swap(low), high)
    side = wide_ref[pl.ds(pl.multiple_of(row0, STEP), span)]
    in_first_row = first((span, lanes))
    u_row = jnp.where(in_first_row, side, swap(side))
    v_row = jnp.where(in_first_row, swap(side), side)
    row_pos = row0 - STEP + lax.broadcasted_iota(jnp.int32, (span, lanes), 0)
    row_in = jnp.where((row_pos >= 0) & (row_pos < bins), 1.0, 0.0)

    def activate(m, carry):
        u_total, v_total = carry
        at = pl.ds(pl.multiple_of(m * STEP, STEP), STEP)
        shape = (STEP, 1, lanes)
        pos = col0 - STEP + m * STEP + lax.broadcasted_iota(jnp.int32, shape, 0)
        pos = pos + jnp.where(first(shape), 0, half)
        col_in = jnp.where((pos >= 0) & (pos < bins), 1.0, 0.0)
        u_col = refs.u_col[at][:, None, :]
        pairs = u_col * u_row[None] + refs.v_col[at][:, None, :] + v_row[None]
        s = 0.5 * jnp.tanh(0.5 * pairs) + 0.5
        s = s * (col_in * row_in[None])
        act = pairs * s
        act_ref[m] = act.reshape(STEP * span, lanes).astype(jnp.bfloat16)
        grad = grad_ref[m] * (s + act * (1.0 - s))
        refs.u_sum[at] = jnp.sum(grad * u_row[None], axis=1)
        refs.v_sum[at] = jnp.sum(grad, axis=1)
        u_total = u_total + jnp.sum(grad * u_col, axis=0)
        return u_total, v_total + jnp.sum(grad, axis=0)

    nothing = jnp.zeros((span, lanes), jnp.float32)
    u_total, v_total = lax.fori_loop(0, blocks + 2, activate, (nothing, nothing))

    row_part = jnp.where(in_first_row, u_total + swap(u_total), v_total + swap(v_total))
    partial[chunk:size] = row_part
    u_sum, v_sum = refs.u_sum[...], refs.v_sum[...]
    col_ref[:depth] = jnp.where(in_first, u_sum, swap(v_sum))
    col_ref[depth:] = jnp.zeros((half, lanes), jnp.float32)
    col_ref[half:] += jnp.where(in_first, swap(u_sum), v_sum)

    away = lax.rem(owner + n_row - row, n_row) - 1

    def owned_copy(d, target):
        return remote(
            col_ref, refs.from_owned.at[d], refs.send_e.at[0], refs.recv_e.at[d], target, col
        )

    @pl.when(row != owner)
    def _():
        owned_copy(away, owner).start()

    def lay(n):
        return jnp.concatenate([act_ref[n + b] for b in range(3)], axis=1)

    def multiply(n, carry):
        product_ref[...] += lax.dot_general(
            lay(n), turned_ref[n], (((0,), (0,)), ((), ())), preferred_element_type=jnp.float32
        )
        return carry

    lax.fori_loop(0, blocks, multiply, 0)
    for a in range(3):
        for b in range(3):
            block = product_ref[b * lanes : (b + 1) * lanes, a * lanes : (a + 1) * lanes]
            tap = (3 * a + b) * channels
            refs.flat[tap : tap + channels] = (
                block[:channels, :channels] + block[channels:, channels:]
            )
    taps = 9 * channels // 2
    refs.packed[:taps] = jnp.concatenate([refs.flat[:taps], refs.flat[taps:]], axis=1)
    if n_row * chunk > taps:
        refs.packed[taps:] = jnp.zeros((n_row * chunk - taps, lanes), jnp.float32)
    to_row = [
        remote(
            refs.packed.at[rows_at(peer, chunk)],
            refs.from_row.at[d],
            refs.send_a.at[d],
            refs.recv_a.at[d],
            peer,
            col,
        )
        for d, peer in enumerate(row_peers)
    ]
    start(to_row)

    def predict(n, carry):
        out = jnp.dot(lay(n), weight_ref[...], preferred_element_type=jnp.float32)
        out = out.reshape(STEP, span, 3 * lanes)
        out = (
            out[:, :rows, :lanes]
            + out[:, STEP : STEP + rows, lanes : 2 * lanes]
            + out[:, 2 * STEP :, 2 * lanes :]
        )
        for k in range(STEP):
            at = n * STEP + k
            turned = out[k].T
            pred_ref[at] = turned[:channels]
            pred_ref[half + at] = turned[channels:]
        start([pred_copy(n, h) for h in range(2)])
        return carry

    bounds = [blocks * part // 4 for part in (0, 1, 2, 4)]
    lax.fori_loop(bounds[0], bounds[1], predict, 0)

    @pl.when(row == owner)
    def _():
        mine = col_ref[...]
        for d in range(n_row - 1):
            owned_copy(d, row_peers[0]).wait_recv()
            mine = mine + refs.from_owned[d]
        begin = chunk + lax.rem(col, ratio) * columns
        partial[pl.ds(pl.multiple_of(begin, STEP), columns + 2 * STEP)] += mine

    @pl.when(row != owner)
    def _():
        owned_copy(away, owner).wait_send()

    wait(to_row)
    mine = refs.packed[rows_at(row, chunk)]
    for d in range(n_row - 1):
        mine = mine + refs.from_row[d]
    partial[:chunk] = mine

    to_col = [
        remote(
            partial.at[rows_at(peer, piece)],
            refs.from_col.at[d],
            refs.send_b.at[d],
            refs.recv_b.at[d],
            row,
            peer,
        )
        for d, peer in enumerate(col_peers)
    ]
    start(to_col)
    lax.fori_loop(bounds[1], bounds[2], predict, 0)
    wait(to_col)
    here = rows_at(col, piece)
    mine = partial[here]
    for d in range(n_col - 1):
        mine = mine + refs.from_col[d]
    total[here] = mine

    back_col = [
        remote(total.at[here], total.at[here], refs.send_c.at[d], refs.recv_c.at[d], row, peer)
        for d, peer in enumerate(col_peers)
    ]
    start(back_col)
    lax.fori_loop(bounds[2], bounds[3], predict, 0)
    wait(back_col)

    below, above = lax.rem(row + n_row - 1, n_row), lax.rem(row + 1, n_row)
    here = rows_at(row, chunk)
    last = [
        remote(
            total.at[pl.ds(begin, STEP)],
            refs.border.at[d],
            refs.send_f.at[d],
            refs.recv_f.at[d],
            peer,
            col,
        )
        for d, (peer, begin) in enumerate([(below, chunk), (above, size - STEP)])
    ] + [
        remote(
            total.at[pl.ds(0, chunk)], every.at[here], refs.send_d.at[d], refs.recv_d.at[d], peer, col
        )
        for d, peer in enumerate(row_peers)
    ]
    start(last)
    every[here] = total[:chunk]
    refs.bins_out[...] = total[chunk + STEP : size - STEP]
    wait(last)
    refs.bins_out[rows - STEP :] += refs.border[0]
    refs.bins_out[:STEP] += refs.border[1]
    refs.taps_out[:taps] = every[:taps, :channels]
    refs.taps_out[taps:] = every[:taps, channels:]
    wait([pred_copy(n, h) for n in range(blocks) for h in range(2)])


def finish_kernel(bins, pred_in, taps_in, bins_in, pred_out, taps_out, bins_out, sem):
    parts = sem.shape[0]
    count = pred_in.shape[0] // parts
    copies = []
    for part in range(parts):
        at = pl.ds(part * count, count)
        copy = pltpu.make_async_copy(pred_in.at[at], pred_out.at[at], sem.at[part])
        copy.start()
        copies.append(copy)
    taps_out[...] = taps_in[...] / bins
    bins_out[...] = bins_in[...] * float(bins) ** (-0.5)
    for copy in copies:
        copy.wait()


def round_up(value, step):
    return -(-value // step) * step


def on_device(n_row, n_col, embedding, kernel, cotangent):
    rows, columns, channels = cotangent.shape
    lanes = 2 * channels
    bins = n_row * rows
    half = columns // 2
    blocks = half // STEP
    span = rows + 2 * STEP
    depth = half + 2 * STEP
    taps = 9 * channels
    chunk = round_up(-(-taps // (2 * n_row)), STEP)
    piece = round_up(-(-(chunk + span) // n_col), STEP)
    f32, bf16 = jnp.float32, jnp.bfloat16
    dma = pltpu.SemaphoreType.DMA
    outputs = {
        "pred_hbm": jax.ShapeDtypeStruct((columns, channels, rows), f32),
        "taps_out": jax.ShapeDtypeStruct((taps, channels), f32),
        "bins_out": jax.ShapeDtypeStruct((rows, lanes), f32),
    }
    scratch = {
        "emb": pltpu.VMEM((rows, lanes), bf16),
        "kernel": pltpu.VMEM(kernel.shape, bf16),
        "cot": pltpu.VMEM((columns, channels, rows), bf16),
        "pred": pltpu.VMEM((columns, channels, rows), f32),
        "held": pltpu.VMEM((n_row - 1, rows, lanes), bf16),
        "wide": pltpu.VMEM((bins + 2 * STEP, lanes), f32),
        "weight": pltpu.VMEM((3 * lanes, 3 * lanes), bf16),
        "u_col": pltpu.VMEM((depth, lanes), f32),
        "v_col": pltpu.VMEM((depth, lanes), f32),
        "act": pltpu.VMEM((blocks + 2, STEP * span, lanes), bf16),
        "turned": pltpu.VMEM((blocks, STEP * span, 3 * lanes), bf16),
        "grad": pltpu.VMEM((blocks + 2, STEP, span, lanes), f32),
        "product": pltpu.VMEM((3 * lanes, 3 * lanes), f32),
        "u_sum": pltpu.VMEM((depth, lanes), f32),
        "v_sum": pltpu.VMEM((depth, lanes), f32),
        "flat": pltpu.VMEM((taps, channels), f32),
        "packed": pltpu.VMEM((n_row * chunk, lanes), f32),
        "col": pltpu.VMEM((columns + 2 * STEP, lanes), f32),
        "from_row": pltpu.VMEM((n_row - 1, chunk, lanes), f32),
        "from_owned": pltpu.VMEM((n_row - 1, columns + 2 * STEP, lanes), f32),
        "partial": pltpu.VMEM((n_col * piece, lanes), f32),
        "from_col": pltpu.VMEM((n_col - 1, piece, lanes), f32),
        "total": pltpu.VMEM((n_col * piece, lanes), f32),
        "every": pltpu.VMEM((n_row * chunk, lanes), f32),
        "border": pltpu.VMEM((2, STEP, lanes), f32),
        "in_sem": dma((2,)),
        "cot_sem": dma((blocks, 2)),
        "pred_sem": dma((blocks, 2)),
        "send_g": dma((n_row - 1,)),
        "recv_g": dma((n_row - 1,)),
        "send_a": dma((n_row - 1,)),
        "recv_a": dma((n_row - 1,)),
        "send_b": dma((n_col - 1,)),
        "recv_b": dma((n_col - 1,)),
        "send_c": dma((n_col - 1,)),
        "recv_c": dma((n_col - 1,)),
        "send_d": dma((n_row - 1,)),
        "recv_d": dma((n_row - 1,)),
        "send_e": dma((1,)),
        "recv_e": dma((n_row - 1,)),
        "send_f": dma((2,)),
        "recv_f": dma((2,)),
    }
    names = ["emb_hbm", "kernel_hbm", "cot_hbm", *outputs, *scratch]

    def tile(*refs):
        tile_kernel(n_row, n_col, chunk, piece, types.SimpleNamespace(**dict(zip(names, refs))))

    prediction, grad_kernel, grad_bins = pl.pallas_call(
        tile,
        out_shape=tuple(outputs.values()),
        in_specs=[ANY, ANY, ANY],
        out_specs=(ANY, VMEM, VMEM),
        scratch_shapes=list(scratch.values()),
        compiler_params=pltpu.CompilerParams(
            collective_id=0, has_side_effects=True, vmem_limit_bytes=60 * 2**20
        ),
        name="tile_gradients",
    )(embedding, kernel, cotangent.transpose(1, 2, 0))

    prediction, grad_kernel, grad_bins = pl.pallas_call(
        functools.partial(finish_kernel, bins),
        out_shape=tuple(outputs.values()),
        in_specs=[ANY, VMEM, VMEM],
        out_specs=(ANY, VMEM, VMEM),
        scratch_shapes=[dma((8,))],
        compiler_params=pltpu.CompilerParams(vmem_limit_bytes=60 * 2**20),
        name="finish",
    )(prediction, grad_kernel, grad_bins)
    return prediction.transpose(2, 0, 1), grad_kernel.reshape(kernel.shape), grad_bins


def solution(mesh):
    in_specs = (P("row", None), P(), P("row", "col", None))
    out_specs = (P("row", "col", None), P(), P("row", None))
    return jax.shard_map(
        functools.partial(on_device, mesh.shape["row"], mesh.shape["col"]),
        mesh=mesh,
        in_specs=in_specs,
        out_specs=out_specs,
        check_vma=False,
    )
```

time: 350 us -> 100 us (0.29)
  waiting for transfers between devices: 227 us -> 0 us
  Pallas kernels: 0 us -> 99.2 us
  matrix products: 41.3 us -> 0 us
  blocking collectives: 24.9 us -> 0 us
  starting transfers between devices: 19.9 us -> 0 us
  between operations: 14.2 us -> 0.64 us
  other arithmetic: 13 us -> 0 us
  local copies, waits for them, and re-layouts: 8.92 us -> 0 us
    psum x3 -> x0, waiting for transfers between devices: 216 us -> none  [the longest x1 73 us: from_root(): return lax.psum(jnp.where(mine, shard, jnp.zeros_like(shard)), axis)]
    pallas_call x0 -> x2, Pallas kernels: none -> 99.2 us  [the longest x1 66.4 us: on_device(): pl.pallas_call(functools.partial(finish_kernel, bins), out_shape=tuple(ou...]
    dot_general x27 -> x0, matrix products: 41.3 us -> none  [the longest x9 23.3 us: on_device(): jnp.einsum('ijc,cd->ijd', shifted_pairs, kernel[kernel_tap_row, kernel_ta...]
    psum x2 -> x0, blocking collectives: 24.9 us -> none  [the longest x1 12.7 us: from_root(): return lax.psum(jnp.where(mine, shard, jnp.zeros_like(shard)), axis)]
    ppermute x8 -> x0, starting transfers between devices: 19.6 us -> none  [the longest x4 14.3 us: padded(): lax.ppermute(tail, axis, [(i, (i + 1) % count) for i in range(ends)])]
    ppermute x8 -> x0, waiting for transfers between devices: 10.6 us -> none  [the longest x4 6.97 us: padded(): lax.ppermute(tail, axis, [(i, (i + 1) % count) for i in range(ends)])]
    add x1 -> x0, other arithmetic: 4.19 us -> none  [build_pairs(): row_embedding[:, None, :channels] * col_embed[None, :, :channels]]
    concatenate x4 -> x0, other arithmetic: 3.88 us -> none  [the longest x2 3.23 us: padded(): jnp.concatenate([lax.ppermute(tail, axis, [(i, (i + 1) % count) for i in...]
  transfers between devices with their start and end apart: 11 -> 0, of which waited for: 5 -> 0; matrix products, arithmetic and copies ran while one was open for 17% -> 0% of each run, Pallas kernels for 0% -> 0%
where the time goes in v3:
time: 100 us; the launch traced here: 99.9 us
  Pallas kernels  99.2 us (99%)
    pallas_call x1, Pallas kernels, on_device(): pl.pallas_call(functools.partial(finish_kernel, bins), out_shape=tuple(ou...  66.4 us
    pallas_call x1, Pallas kernels, on_device(): pl.pallas_call(tile, out_shape=tuple(outputs.values()), in_specs=[ANY, AN...  32.8 us

profile of v3, /device:TPU:0, one launch (start us, length us, event | category | flops | bytes accessed | tf_op | source)
XLA Modules:
  0.0 99.9 jit_solution(7804727759638908812)
XLA Ops:
  0.6 32.8 %tile_gradients.1 = (f32[64,64,128]{2,1,0:T(8,128)}, f32[576,64]{1,0:T(8,128)}, f32[128,128]{1,0:T(8,128)}) custom-call(bf16[128,128]{1,0:T(8,128)(2,1)} %refs_0_.1, bf16[3,3,64,64]{3,2,1,0:T(8,128)(2,1)} %refs_1_.1, bf16[64,64,128]{2,1,0:T(8,128)(2,1)} %bitcast.3), custom_call_target="tpu_custom_call" | custom-call | tf_op jit(solution)/shard_map/tile_gradients/pallas_call | solution.py:417
  33.5 66.4 %finish.1 = (f32[64,64,128]{2,1,0:T(8,128)}, f32[576,64]{1,0:T(8,128)}, f32[128,128]{1,0:T(8,128)}) custom-call(f32[64,64,128]{2,1,0:T(8,128)} %get-tuple-element.9.pred_in, f32[576,64]{1,0:T(8,128)} %get-tuple-element.10.taps_in, f32[128,128]{1,0:T(8,128)} %get-tuple-element.11.bins_in), custom_call_target="tpu_custom_call" | custom-call | tf_op jit(solution)/shard_map/finish/pallas_call | solution.py:429

commit v4 on v3

--- a/solution.py
+++ b/solution.py
@@ -328,18 +328,24 @@
     wait([pred_copy(n, h) for n in range(blocks) for h in range(2)])
 
 
-def finish_kernel(bins, pred_in, taps_in, bins_in, pred_out, taps_out, bins_out, sem):
-    parts = sem.shape[0]
+def finish_kernel(bins, pred_in, taps_in, bins_in, pred_out, taps_out, bins_out, held, sem):
+    parts = sem.shape[1]
     count = pred_in.shape[0] // parts
     copies = []
     for part in range(parts):
         at = pl.ds(part * count, count)
-        copy = pltpu.make_async_copy(pred_in.at[at], pred_out.at[at], sem.at[part])
+        copy = pltpu.make_async_copy(pred_in.at[at], held.at[at], sem.at[0, part])
         copy.start()
         copies.append(copy)
     taps_out[...] = taps_in[...] / bins
     bins_out[...] = bins_in[...] * float(bins) ** (-0.5)
-    for copy in copies:
+    for part in range(parts):
+        copies[part].wait()
+        at = pl.ds(part * count, count)
+        copy = pltpu.make_async_copy(held.at[at], pred_out.at[at], sem.at[1, part])
+        copy.start()
+        copies.append(copy)
+    for copy in copies[parts:]:
         copy.wait()
 
 
@@ -431,7 +437,7 @@
         out_shape=tuple(outputs.values()),
         in_specs=[ANY, VMEM, VMEM],
         out_specs=(ANY, VMEM, VMEM),
-        scratch_shapes=[dma((8,))],
+        scratch_shapes=[pltpu.VMEM((columns, channels, rows), f32), dma((2, 8))],
         compiler_params=pltpu.CompilerParams(vmem_limit_bytes=60 * 2**20),
         name="finish",
     )(prediction, grad_kernel, grad_bins)

time: 100 us -> 37.7 us (0.38)
  Pallas kernels: 99.2 us -> 36.9 us
    pallas_call x1, Pallas kernels: 66.4 us -> 4.09 us  [on_device(): pl.pallas_call(functools.partial(finish_kernel, bins), out_shape=tuple(ou...]
where the time goes in v4:
time: 37.7 us; the launch traced here: 37.6 us
  Pallas kernels  36.9 us (98%)
  between operations  0.64 us (2%)
    pallas_call x1, Pallas kernels, on_device(): pl.pallas_call(tile, out_shape=tuple(outputs.values()), in_specs=[ANY, AN...  32.8 us
    pallas_call x1, Pallas kernels, on_device(): pl.pallas_call(functools.partial(finish_kernel, bins), out_shape=tuple(ou...  4.09 us

profile of v4, /device:TPU:0, one launch (start us, length us, event | category | flops | bytes accessed | tf_op | source)
XLA Modules:
  0.0 37.6 jit_solution(6878466259198491287)
XLA Ops:
  0.6 32.8 %tile_gradients.1 = (f32[64,64,128]{2,1,0:T(8,128)}, f32[576,64]{1,0:T(8,128)}, f32[128,128]{1,0:T(8,128)}) custom-call(bf16[128,128]{1,0:T(8,128)(2,1)} %refs_0_.1, bf16[3,3,64,64]{3,2,1,0:T(8,128)(2,1)} %refs_1_.1, bf16[64,64,128]{2,1,0:T(8,128)(2,1)} %bitcast.3), custom_call_target="tpu_custom_call" | custom-call | tf_op jit(solution)/shard_map/tile_gradients/pallas_call | solution.py:423
  33.5 4.1 %finish.1 = (f32[64,64,128]{2,1,0:T(8,128)}, f32[576,64]{1,0:T(8,128)}, f32[128,128]{1,0:T(8,128)}) custom-call(f32[64,64,128]{2,1,0:T(8,128)} %get-tuple-element.9.pred_in, f32[576,64]{1,0:T(8,128)} %get-tuple-element.10.taps_in, f32[128,128]{1,0:T(8,128)} %get-tuple-element.11.bins_in), custom_call_target="tpu_custom_call" | custom-call | tf_op jit(solution)/shard_map/finish/pallas_call | solution.py:435

commit v5 on v3

--- a/solution.py
+++ b/solution.py
@@ -11,7 +11,7 @@
 STEP = 8
 MESH = pl.DeviceIdType.MESH
 VMEM = pl.BlockSpec(memory_space=pltpu.VMEM)
-ANY = pl.BlockSpec(memory_space=pl.ANY)
+HBM = pl.BlockSpec(memory_space=pltpu.HBM)
 
 
 def signal(barrier, row, col):
@@ -55,10 +55,6 @@
     def cot_copy(n, h):
         at = pl.ds(h * half + n * STEP, STEP)
         return local(cot_hbm.at[at], cot_ref.at[at], refs.cot_sem.at[n, h])
-
-    def pred_copy(n, h):
-        at = pl.ds(h * half + n * STEP, STEP)
-        return local(pred_ref.at[at], refs.pred_hbm.at[at], refs.pred_sem.at[n, h])
 
     def rows_at(index, count):
         return pl.ds(pl.multiple_of(index * count, STEP), count)
@@ -246,7 +242,6 @@
             turned = out[k].T
             pred_ref[at] = turned[:channels]
             pred_ref[half + at] = turned[channels:]
-        start([pred_copy(n, h) for h in range(2)])
         return carry
 
     bounds = [blocks * part // 4 for part in (0, 1, 2, 4)]
@@ -325,22 +320,27 @@
     refs.bins_out[:STEP] += refs.border[1]
     refs.taps_out[:taps] = every[:taps, :channels]
     refs.taps_out[taps:] = every[:taps, channels:]
-    wait([pred_copy(n, h) for n in range(blocks) for h in range(2)])
-
-
-def finish_kernel(bins, pred_in, taps_in, bins_in, pred_out, taps_out, bins_out, sem):
-    parts = sem.shape[0]
-    count = pred_in.shape[0] // parts
-    copies = []
-    for part in range(parts):
-        at = pl.ds(part * count, count)
-        copy = pltpu.make_async_copy(pred_in.at[at], pred_out.at[at], sem.at[part])
-        copy.start()
-        copies.append(copy)
-    taps_out[...] = taps_in[...] / bins
-    bins_out[...] = bins_in[...] * float(bins) ** (-0.5)
+
+
+def finish_kernel(
+    bins, pred_in, taps_in, bins_in, pred_out, taps_out, bins_out, taps_ref, bins_ref, sem
+):
+    copies = [
+        pltpu.make_async_copy(pred_in, pred_out, sem.at[0]),
+        pltpu.make_async_copy(taps_ref, taps_out, sem.at[1]),
+        pltpu.make_async_copy(bins_ref, bins_out, sem.at[2]),
+    ]
+    copies[0].start()
+    taps_ref[...] = taps_in[...] / bins
+    copies[1].start()
+    bins_ref[...] = bins_in[...] * float(bins) ** (-0.5)
+    copies[2].start()
     for copy in copies:
         copy.wait()
+
+
+def in_hbm(x):
+    return pltpu.with_memory_space_constraint(x, pltpu.HBM)
 
 
 def round_up(value, step):
@@ -361,7 +361,7 @@
     f32, bf16 = jnp.float32, jnp.bfloat16
     dma = pltpu.SemaphoreType.DMA
     outputs = {
-        "pred_hbm": jax.ShapeDtypeStruct((columns, channels, rows), f32),
+        "pred": jax.ShapeDtypeStruct((columns, channels, rows), f32),
         "taps_out": jax.ShapeDtypeStruct((taps, channels), f32),
         "bins_out": jax.ShapeDtypeStruct((rows, lanes), f32),
     }
@@ -369,7 +369,6 @@
         "emb": pltpu.VMEM((rows, lanes), bf16),
         "kernel": pltpu.VMEM(kernel.shape, bf16),
         "cot": pltpu.VMEM((columns, channels, rows), bf16),
-        "pred": pltpu.VMEM((columns, channels, rows), f32),
         "held": pltpu.VMEM((n_row - 1, rows, lanes), bf16),
         "wide": pltpu.VMEM((bins + 2 * STEP, lanes), f32),
         "weight": pltpu.VMEM((3 * lanes, 3 * lanes), bf16),
@@ -393,7 +392,6 @@
         "border": pltpu.VMEM((2, STEP, lanes), f32),
         "in_sem": dma((2,)),
         "cot_sem": dma((blocks, 2)),
-        "pred_sem": dma((blocks, 2)),
         "send_g": dma((n_row - 1,)),
         "recv_g": dma((n_row - 1,)),
         "send_a": dma((n_row - 1,)),
@@ -417,22 +415,26 @@
     prediction, grad_kernel, grad_bins = pl.pallas_call(
         tile,
         out_shape=tuple(outputs.values()),
-        in_specs=[ANY, ANY, ANY],
-        out_specs=(ANY, VMEM, VMEM),
+        in_specs=[HBM, HBM, HBM],
+        out_specs=(VMEM, VMEM, VMEM),
         scratch_shapes=list(scratch.values()),
         compiler_params=pltpu.CompilerParams(
-            collective_id=0, has_side_effects=True, vmem_limit_bytes=60 * 2**20
+            collective_id=0, has_side_effects=True, vmem_limit_bytes=32 * 2**20
         ),
         name="tile_gradients",
-    )(embedding, kernel, cotangent.transpose(1, 2, 0))
+    )(*[in_hbm(x) for x in (embedding, kernel, cotangent.transpose(1, 2, 0))])
 
     prediction, grad_kernel, grad_bins = pl.pallas_call(
         functools.partial(finish_kernel, bins),
         out_shape=tuple(outputs.values()),
-        in_specs=[ANY, VMEM, VMEM],
-        out_specs=(ANY, VMEM, VMEM),
-        scratch_shapes=[dma((8,))],
-        compiler_params=pltpu.CompilerParams(vmem_limit_bytes=60 * 2**20),
+        in_specs=[VMEM, VMEM, VMEM],
+        out_specs=(HBM, HBM, HBM),
+        scratch_shapes=[
+            pltpu.VMEM((taps, channels), f32),
+            pltpu.VMEM((rows, lanes), f32),
+            dma((3,)),
+        ],
+        compiler_params=pltpu.CompilerParams(vmem_limit_bytes=24 * 2**20),
         name="finish",
     )(prediction, grad_kernel, grad_bins)
     return prediction.transpose(2, 0, 1), grad_kernel.reshape(kernel.shape), grad_bins

time: 100 us -> 34.2 us (0.34)
  Pallas kernels: 99.2 us -> 33.4 us
    pallas_call x1, Pallas kernels: 66.4 us -> 1.45 us  [on_device(): pl.pallas_call(functools.partial(finish_kernel, bins), out_shape=tuple(ou...]
where the time goes in v5:
time: 34.2 us; the launch traced here: 34.1 us
  Pallas kernels  33.4 us (98%)
  between operations  0.64 us (2%)
    pallas_call x1, Pallas kernels, on_device(): pl.pallas_call(tile, out_shape=tuple(outputs.values()), in_specs=[HBM, HB...  32 us
    pallas_call x1, Pallas kernels, on_device(): pl.pallas_call(functools.partial(finish_kernel, bins), out_shape=tuple(ou...  1.45 us

profile of v5, /device:TPU:0, one launch (start us, length us, event | category | flops | bytes accessed | tf_op | source)
XLA Modules:
  0.0 34.1 jit_solution(3147889890547831394)
XLA Ops:
  0.6 32.0 %tile_gradients.1 = (f32[64,64,128]{2,1,0:T(8,128)S(1)}, f32[576,64]{1,0:T(8,128)S(1)}, f32[128,128]{1,0:T(8,128)S(1)}) custom-call(bf16[128,128]{1,0:T(8,128)(2,1)} %refs_0_.1, bf16[3,3,64,64]{3,2,1,0:T(8,128)(2,1)} %refs_1_.1, bf16[64,64,128]{2,1,0:T(8,128)(2,1)} %bitcast.3), custom_call_target="tpu_custom_call" | custom-call | tf_op jit(solution)/shard_map/tile_gradients/pallas_call | solution.py:415
  32.6 1.4 %finish.1 = (f32[64,64,128]{2,1,0:T(8,128)}, f32[576,64]{1,0:T(8,128)}, f32[128,128]{1,0:T(8,128)}) custom-call(f32[64,64,128]{2,1,0:T(8,128)S(1)} %get-tuple-element.9.pred_in, f32[576,64]{1,0:T(8,128)S(1)} %get-tuple-element.10.taps_in, f32[128,128]{1,0:T(8,128)S(1)} %get-tuple-element.11.bins_in), custom_call_target="tpu_custom_call" | custom-call | tf_op jit(solution)/shard_map/finish/pallas_call | solution.py:427

commit v6 on v5

--- a/solution.py
+++ b/solution.py
@@ -29,11 +29,13 @@
     )
 
 
-def tile_kernel(n_row, n_col, chunk, piece, refs):
+def tile_kernel(n_row, n_col, chunk, refs):
     emb_hbm, kernel_hbm, cot_hbm = refs.emb_hbm, refs.kernel_hbm, refs.cot_hbm
     wide_ref, weight_ref, cot_ref, pred_ref = refs.wide, refs.weight, refs.cot, refs.pred
     act_ref, turned_ref, grad_ref, product_ref = refs.act, refs.turned, refs.grad, refs.product
-    col_ref, partial, total, every = refs.col, refs.partial, refs.total, refs.every
+    col_ref, every = refs.col, refs.every
+    bins_sum, taps_sum = refs.bins_sum, refs.taps_sum
+    bins_total, taps_total = refs.bins_total, refs.taps_total
     columns, channels, rows = cot_ref.shape
     half = columns // 2
     blocks = half // STEP
@@ -41,7 +43,6 @@
     depth = half + 2 * STEP
     lanes = 2 * channels
     bins = n_row * rows
-    size = chunk + span
     ratio = rows // columns
     row, col = lax.axis_index("row"), lax.axis_index("col")
     row0, col0 = row * rows, col * columns
@@ -84,8 +85,9 @@
     zeros = jnp.zeros((STEP, lanes), jnp.float32)
     wide_ref[:STEP] = zeros
     wide_ref[STEP + bins :] = zeros
-    if n_col * piece > size:
-        partial[size:] = jnp.zeros((n_col * piece - size, lanes), jnp.float32)
+    for ref, used in [(bins_sum, span), (taps_sum, chunk)]:
+        if ref.shape[0] > used:
+            ref[used:] = jnp.zeros((ref.shape[0] - used, lanes), jnp.float32)
 
     wait(inputs)
     pl.semaphore_wait(barrier, n_row + n_col - 2)
@@ -178,7 +180,7 @@
     u_total, v_total = lax.fori_loop(0, blocks + 2, activate, (nothing, nothing))
 
     row_part = jnp.where(in_first_row, u_total + swap(u_total), v_total + swap(v_total))
-    partial[chunk:size] = row_part
+    bins_sum[:span] = row_part
     u_sum, v_sum = refs.u_sum[...], refs.v_sum[...]
     col_ref[:depth] = jnp.where(in_first, u_sum, swap(v_sum))
     col_ref[depth:] = jnp.zeros((half, lanes), jnp.float32)
@@ -244,8 +246,49 @@
             pred_ref[half + at] = turned[channels:]
         return carry
 
-    bounds = [blocks * part // 4 for part in (0, 1, 2, 4)]
-    lax.fori_loop(bounds[0], bounds[1], predict, 0)
+    def some(part):
+        lax.fori_loop(blocks * part // 4, blocks * (part + 1) // 4, predict, 0)
+
+    def to_owners(source, landing, sems, first_sem):
+        piece = landing.shape[1]
+        return [
+            remote(
+                source.at[rows_at(peer, piece)],
+                landing.at[d],
+                sems[0].at[first_sem + d],
+                sems[1].at[first_sem + d],
+                row,
+                peer,
+            )
+            for d, peer in enumerate(col_peers)
+        ]
+
+    def to_all(source, landing, sems, first_sem):
+        here = rows_at(col, landing.shape[1])
+        return [
+            remote(
+                source.at[here],
+                source.at[here],
+                sems[0].at[first_sem + d],
+                sems[1].at[first_sem + d],
+                row,
+                peer,
+            )
+            for d, peer in enumerate(col_peers)
+        ]
+
+    def add_pieces(source, landing, target):
+        here = rows_at(col, landing.shape[1])
+        mine = source[here]
+        for d in range(n_col - 1):
+            mine = mine + landing[d]
+        target[here] = mine
+
+    out_sems, back_sems = (refs.send_b, refs.recv_b), (refs.send_c, refs.recv_c)
+    bins_out = to_owners(bins_sum, refs.bins_landing, out_sems, 0)
+    taps_out = to_owners(taps_sum, refs.taps_landing, out_sems, n_col - 1)
+    bins_back = to_all(bins_total, refs.bins_landing, back_sems, 0)
+    taps_back = to_all(taps_total, refs.taps_landing, back_sems, n_col - 1)
 
     @pl.when(row == owner)
     def _():
@@ -253,71 +296,66 @@
         for d in range(n_row - 1):
             owned_copy(d, row_peers[0]).wait_recv()
             mine = mine + refs.from_owned[d]
-        begin = chunk + lax.rem(col, ratio) * columns
-        partial[pl.ds(pl.multiple_of(begin, STEP), columns + 2 * STEP)] += mine
+        begin = lax.rem(col, ratio) * columns
+        bins_sum[pl.ds(pl.multiple_of(begin, STEP), columns + 2 * STEP)] += mine
 
     @pl.when(row != owner)
     def _():
         owned_copy(away, owner).wait_send()
 
+    start(bins_out)
+    some(0)
     wait(to_row)
     mine = refs.packed[rows_at(row, chunk)]
     for d in range(n_row - 1):
         mine = mine + refs.from_row[d]
-    partial[:chunk] = mine
-
-    to_col = [
+    taps_sum[:chunk] = mine
+    start(taps_out)
+
+    wait(bins_out)
+    add_pieces(bins_sum, refs.bins_landing, bins_total)
+    start(bins_back)
+    some(1)
+    wait(taps_out)
+    add_pieces(taps_sum, refs.taps_landing, taps_total)
+    start(taps_back)
+    some(2)
+
+    wait(bins_back)
+    below, above = lax.rem(row + n_row - 1, n_row), lax.rem(row + 1, n_row)
+    borders = [
         remote(
-            partial.at[rows_at(peer, piece)],
-            refs.from_col.at[d],
-            refs.send_b.at[d],
-            refs.recv_b.at[d],
-            row,
-            peer,
-        )
-        for d, peer in enumerate(col_peers)
-    ]
-    start(to_col)
-    lax.fori_loop(bounds[1], bounds[2], predict, 0)
-    wait(to_col)
-    here = rows_at(col, piece)
-    mine = partial[here]
-    for d in range(n_col - 1):
-        mine = mine + refs.from_col[d]
-    total[here] = mine
-
-    back_col = [
-        remote(total.at[here], total.at[here], refs.send_c.at[d], refs.recv_c.at[d], row, peer)
-        for d, peer in enumerate(col_peers)
-    ]
-    start(back_col)
-    lax.fori_loop(bounds[2], bounds[3], predict, 0)
-    wait(back_col)
-
-    below, above = lax.rem(row + n_row - 1, n_row), lax.rem(row + 1, n_row)
-    here = rows_at(row, chunk)
-    last = [
-        remote(
-            total.at[pl.ds(begin, STEP)],
+            bins_total.at[pl.ds(begin, STEP)],
             refs.border.at[d],
             refs.send_f.at[d],
             refs.recv_f.at[d],
             peer,
             col,
         )
-        for d, (peer, begin) in enumerate([(below, chunk), (above, size - STEP)])
-    ] + [
+        for d, (peer, begin) in enumerate([(below, 0), (above, span - STEP)])
+    ]
+    start(borders)
+    wait(taps_back)
+    here = rows_at(row, chunk)
+    spread_taps = [
         remote(
-            total.at[pl.ds(0, chunk)], every.at[here], refs.send_d.at[d], refs.recv_d.at[d], peer, col
+            taps_total.at[pl.ds(0, chunk)],
+            every.at[here],
+            refs.send_d.at[d],
+            refs.recv_d.at[d],
+            peer,
+            col,
         )
         for d, peer in enumerate(row_peers)
     ]
-    start(last)
-    every[here] = total[:chunk]
-    refs.bins_out[...] = total[chunk + STEP : size - STEP]
-    wait(last)
+    start(spread_taps)
+    every[here] = taps_total[:chunk]
+    some(3)
+    refs.bins_out[...] = bins_total[STEP : span - STEP]
+    wait(borders)
     refs.bins_out[rows - STEP :] += refs.border[0]
     refs.bins_out[:STEP] += refs.border[1]
+    wait(spread_taps)
     refs.taps_out[:taps] = every[:taps, :channels]
     refs.taps_out[taps:] = every[:taps, channels:]
 
@@ -357,7 +395,8 @@
     depth = half + 2 * STEP
     taps = 9 * channels
     chunk = round_up(-(-taps // (2 * n_row)), STEP)
-    piece = round_up(-(-(chunk + span) // n_col), STEP)
+    taps_piece = round_up(-(-chunk // n_col), STEP)
+    bins_piece = round_up(-(-span // n_col), STEP)
     f32, bf16 = jnp.float32, jnp.bfloat16
     dma = pltpu.SemaphoreType.DMA
     outputs = {
@@ -385,9 +424,12 @@
         "col": pltpu.VMEM((columns + 2 * STEP, lanes), f32),
         "from_row": pltpu.VMEM((n_row - 1, chunk, lanes), f32),
         "from_owned": pltpu.VMEM((n_row - 1, columns + 2 * STEP, lanes), f32),
-        "partial": pltpu.VMEM((n_col * piece, lanes), f32),
-        "from_col": pltpu.VMEM((n_col - 1, piece, lanes), f32),
-        "total": pltpu.VMEM((n_col * piece, lanes), f32),
+        "bins_sum": pltpu.VMEM((n_col * bins_piece, lanes), f32),
+        "bins_landing": pltpu.VMEM((n_col - 1, bins_piece, lanes), f32),
+        "bins_total": pltpu.VMEM((n_col * bins_piece, lanes), f32),
+        "taps_sum": pltpu.VMEM((n_col * taps_piece, lanes), f32),
+        "taps_landing": pltpu.VMEM((n_col - 1, taps_piece, lanes), f32),
+        "taps_total": pltpu.VMEM((n_col * taps_piece, lanes), f32),
         "every": pltpu.VMEM((n_row * chunk, lanes), f32),
         "border": pltpu.VMEM((2, STEP, lanes), f32),
         "in_sem": dma((2,)),
@@ -396,10 +438,10 @@
         "recv_g": dma((n_row - 1,)),
         "send_a": dma((n_row - 1,)),
         "recv_a": dma((n_row - 1,)),
-        "send_b": dma((n_col - 1,)),
-        "recv_b": dma((n_col - 1,)),
-        "send_c": dma((n_col - 1,)),
-        "recv_c": dma((n_col - 1,)),
+        "send_b": dma((2 * (n_col - 1),)),
+        "recv_b": dma((2 * (n_col - 1),)),
+        "send_c": dma((2 * (n_col - 1),)),
+        "recv_c": dma((2 * (n_col - 1),)),
         "send_d": dma((n_row - 1,)),
         "recv_d": dma((n_row - 1,)),
         "send_e": dma((1,)),
@@ -410,7 +452,7 @@
     names = ["emb_hbm", "kernel_hbm", "cot_hbm", *outputs, *scratch]
 
     def tile(*refs):
-        tile_kernel(n_row, n_col, chunk, piece, types.SimpleNamespace(**dict(zip(names, refs))))
+        tile_kernel(n_row, n_col, chunk, types.SimpleNamespace(**dict(zip(names, refs))))
 
     prediction, grad_kernel, grad_bins = pl.pallas_call(
         tile,

time: 34.2 us -> 33.7 us (0.985)
  Pallas kernels: 33.4 us -> 32.9 us
    pallas_call x1, Pallas kernels: 32 us -> 31.5 us  [on_device(): pl.pallas_call(tile, out_shape=tuple(outputs.values()), in_specs=[HBM, HB...]
where the time goes in v6:
time: 33.7 us; the launch traced here: 33.5 us
  Pallas kernels  32.9 us (98%)
  between operations  0.64 us (2%)
    pallas_call x1, Pallas kernels, on_device(): pl.pallas_call(tile, out_shape=tuple(outputs.values()), in_specs=[HBM, HB...  31.5 us
    pallas_call x1, Pallas kernels, on_device(): pl.pallas_call(functools.partial(finish_kernel, bins), out_shape=tuple(ou...  1.45 us

profile of v6, /device:TPU:0, one launch (start us, length us, event | category | flops | bytes accessed | tf_op | source)
XLA Modules:
  0.0 33.5 jit_solution(12941128710294132385)
XLA Ops:
  0.6 31.5 %tile_gradients.1 = (f32[64,64,128]{2,1,0:T(8,128)S(1)}, f32[576,64]{1,0:T(8,128)S(1)}, f32[128,128]{1,0:T(8,128)S(1)}) custom-call(bf16[128,128]{1,0:T(8,128)(2,1)} %refs_0_.1, bf16[3,3,64,64]{3,2,1,0:T(8,128)(2,1)} %refs_1_.1, bf16[64,64,128]{2,1,0:T(8,128)(2,1)} %bitcast.3), custom_call_target="tpu_custom_call" | custom-call | tf_op jit(solution)/shard_map/tile_gradients/pallas_call | solution.py:457
  32.1 1.4 %finish.1 = (f32[64,64,128]{2,1,0:T(8,128)}, f32[576,64]{1,0:T(8,128)}, f32[128,128]{1,0:T(8,128)}) custom-call(f32[64,64,128]{2,1,0:T(8,128)S(1)} %get-tuple-element.9.pred_in, f32[576,64]{1,0:T(8,128)S(1)} %get-tuple-element.10.taps_in, f32[128,128]{1,0:T(8,128)S(1)} %get-tuple-element.11.bins_in), custom_call_target="tpu_custom_call" | custom-call | tf_op jit(solution)/shard_map/finish/pallas_call | solution.py:469

commit v7 on v6

--- a/solution.py
+++ b/solution.py
@@ -85,7 +85,7 @@
     zeros = jnp.zeros((STEP, lanes), jnp.float32)
     wide_ref[:STEP] = zeros
     wide_ref[STEP + bins :] = zeros
-    for ref, used in [(bins_sum, span), (taps_sum, chunk)]:
+    for ref, used in [(bins_sum, rows), (taps_sum, chunk + 2 * STEP)]:
         if ref.shape[0] > used:
             ref[used:] = jnp.zeros((ref.shape[0] - used, lanes), jnp.float32)
 
@@ -180,7 +180,7 @@
     u_total, v_total = lax.fori_loop(0, blocks + 2, activate, (nothing, nothing))
 
     row_part = jnp.where(in_first_row, u_total + swap(u_total), v_total + swap(v_total))
-    bins_sum[:span] = row_part
+    refs.row[...] = row_part
     u_sum, v_sum = refs.u_sum[...], refs.v_sum[...]
     col_ref[:depth] = jnp.where(in_first, u_sum, swap(v_sum))
     col_ref[depth:] = jnp.zeros((half, lanes), jnp.float32)
@@ -297,12 +297,15 @@
             owned_copy(d, row_peers[0]).wait_recv()
             mine = mine + refs.from_owned[d]
         begin = lax.rem(col, ratio) * columns
-        bins_sum[pl.ds(pl.multiple_of(begin, STEP), columns + 2 * STEP)] += mine
+        refs.row[pl.ds(pl.multiple_of(begin, STEP), columns + 2 * STEP)] += mine
 
     @pl.when(row != owner)
     def _():
         owned_copy(away, owner).wait_send()
 
+    bins_sum[:rows] = refs.row[STEP : STEP + rows]
+    taps_sum[chunk : chunk + STEP] = refs.row[:STEP]
+    taps_sum[chunk + STEP : chunk + 2 * STEP] = refs.row[STEP + rows :]
     start(bins_out)
     some(0)
     wait(to_row)
@@ -321,21 +324,20 @@
     start(taps_back)
     some(2)
 
-    wait(bins_back)
+    wait(taps_back)
     below, above = lax.rem(row + n_row - 1, n_row), lax.rem(row + 1, n_row)
     borders = [
         remote(
-            bins_total.at[pl.ds(begin, STEP)],
+            taps_total.at[pl.ds(chunk + d * STEP, STEP)],
             refs.border.at[d],
             refs.send_f.at[d],
             refs.recv_f.at[d],
             peer,
             col,
         )
-        for d, (peer, begin) in enumerate([(below, 0), (above, span - STEP)])
+        for d, peer in enumerate([below, above])
     ]
     start(borders)
-    wait(taps_back)
     here = rows_at(row, chunk)
     spread_taps = [
         remote(
@@ -351,7 +353,8 @@
     start(spread_taps)
     every[here] = taps_total[:chunk]
     some(3)
-    refs.bins_out[...] = bins_total[STEP : span - STEP]
+    wait(bins_back)
+    refs.bins_out[...] = bins_total[:rows]
     wait(borders)
     refs.bins_out[rows - STEP :] += refs.border[0]
     refs.bins_out[:STEP] += refs.border[1]
@@ -395,8 +398,8 @@
     depth = half + 2 * STEP
     taps = 9 * channels
     chunk = round_up(-(-taps // (2 * n_row)), STEP)
-    taps_piece = round_up(-(-chunk // n_col), STEP)
-    bins_piece = round_up(-(-span // n_col), STEP)
+    taps_piece = round_up(-(-(chunk + 2 * STEP) // n_col), STEP)
+    bins_piece = round_up(-(-rows // n_col), STEP)
     f32, bf16 = jnp.float32, jnp.bfloat16
     dma = pltpu.SemaphoreType.DMA
     outputs = {
@@ -424,6 +427,7 @@
         "col": pltpu.VMEM((columns + 2 * STEP, lanes), f32),
         "from_row": pltpu.VMEM((n_row - 1, chunk, lanes), f32),
         "from_owned": pltpu.VMEM((n_row - 1, columns + 2 * STEP, lanes), f32),
+        "row": pltpu.VMEM((span, lanes), f32),
         "bins_sum": pltpu.VMEM((n_col * bins_piece, lanes), f32),
         "bins_landing": pltpu.VMEM((n_col - 1, bins_piece, lanes), f32),
         "bins_total": pltpu.VMEM((n_col * bins_piece, lanes), f32),

time: 33.7 us -> 33.7 us (level)
  no operation moved by 1% of the time
where the time goes in v7:
time: 33.7 us; the launch traced here: 33.5 us
  Pallas kernels  32.9 us (98%)
  between operations  0.64 us (2%)
    pallas_call x1, Pallas kernels, on_device(): pl.pallas_call(tile, out_shape=tuple(outputs.values()), in_specs=[HBM, HB...  31.4 us
    pallas_call x1, Pallas kernels, on_device(): pl.pallas_call(functools.partial(finish_kernel, bins), out_shape=tuple(ou...  1.45 us

profile of v7, /device:TPU:0, one launch (start us, length us, event | category | flops | bytes accessed | tf_op | source)
XLA Modules:
  0.0 33.5 jit_solution(8187132969362147726)
XLA Ops:
  0.6 31.4 %tile_gradients.1 = (f32[64,64,128]{2,1,0:T(8,128)S(1)}, f32[576,64]{1,0:T(8,128)S(1)}, f32[128,128]{1,0:T(8,128)S(1)}) custom-call(bf16[128,128]{1,0:T(8,128)(2,1)} %refs_0_.1, bf16[3,3,64,64]{3,2,1,0:T(8,128)(2,1)} %refs_1_.1, bf16[64,64,128]{2,1,0:T(8,128)(2,1)} %bitcast.3), custom_call_target="tpu_custom_call" | custom-call | tf_op jit(solution)/shard_map/tile_gradients/pallas_call | solution.py:461
  32.1 1.4 %finish.1 = (f32[64,64,128]{2,1,0:T(8,128)}, f32[576,64]{1,0:T(8,128)}, f32[128,128]{1,0:T(8,128)}) custom-call(f32[64,64,128]{2,1,0:T(8,128)S(1)} %get-tuple-element.9.pred_in, f32[576,64]{1,0:T(8,128)S(1)} %get-tuple-element.10.taps_in, f32[128,128]{1,0:T(8,128)S(1)} %get-tuple-element.11.bins_in), custom_call_target="tpu_custom_call" | custom-call | tf_op jit(solution)/shard_map/finish/pallas_call | solution.py:473

commit v8 on v7

--- a/solution.py
+++ b/solution.py
@@ -158,7 +158,6 @@
     row_in = jnp.where((row_pos >= 0) & (row_pos < bins), 1.0, 0.0)
 
     def activate(m, carry):
-        u_total, v_total = carry
         at = pl.ds(pl.multiple_of(m * STEP, STEP), STEP)
         shape = (STEP, 1, lanes)
         pos = col0 - STEP + m * STEP + lax.broadcasted_iota(jnp.int32, shape, 0)
@@ -170,32 +169,10 @@
         s = s * (col_in * row_in[None])
         act = pairs * s
         act_ref[m] = act.reshape(STEP * span, lanes).astype(jnp.bfloat16)
-        grad = grad_ref[m] * (s + act * (1.0 - s))
-        refs.u_sum[at] = jnp.sum(grad * u_row[None], axis=1)
-        refs.v_sum[at] = jnp.sum(grad, axis=1)
-        u_total = u_total + jnp.sum(grad * u_col, axis=0)
-        return u_total, v_total + jnp.sum(grad, axis=0)
-
-    nothing = jnp.zeros((span, lanes), jnp.float32)
-    u_total, v_total = lax.fori_loop(0, blocks + 2, activate, (nothing, nothing))
-
-    row_part = jnp.where(in_first_row, u_total + swap(u_total), v_total + swap(v_total))
-    refs.row[...] = row_part
-    u_sum, v_sum = refs.u_sum[...], refs.v_sum[...]
-    col_ref[:depth] = jnp.where(in_first, u_sum, swap(v_sum))
-    col_ref[depth:] = jnp.zeros((half, lanes), jnp.float32)
-    col_ref[half:] += jnp.where(in_first, swap(u_sum), v_sum)
-
-    away = lax.rem(owner + n_row - row, n_row) - 1
-
-    def owned_copy(d, target):
-        return remote(
-            col_ref, refs.from_owned.at[d], refs.send_e.at[0], refs.recv_e.at[d], target, col
-        )
-
-    @pl.when(row != owner)
-    def _():
-        owned_copy(away, owner).start()
+        refs.slope[m] = s + act * (1.0 - s)
+        return carry
+
+    lax.fori_loop(0, blocks + 2, activate, 0)
 
     def lay(n):
         return jnp.concatenate([act_ref[n + b] for b in range(3)], axis=1)
@@ -231,6 +208,36 @@
     ]
     start(to_row)
 
+    def reduce(m, carry):
+        u_total, v_total = carry
+        at = pl.ds(pl.multiple_of(m * STEP, STEP), STEP)
+        grad = grad_ref[m] * refs.slope[m]
+        refs.u_sum[at] = jnp.sum(grad * u_row[None], axis=1)
+        refs.v_sum[at] = jnp.sum(grad, axis=1)
+        u_total = u_total + jnp.sum(grad * refs.u_col[at][:, None, :], axis=0)
+        return u_total, v_total + jnp.sum(grad, axis=0)
+
+    nothing = jnp.zeros((span, lanes), jnp.float32)
+    u_total, v_total = lax.fori_loop(0, blocks + 2, reduce, (nothing, nothing))
+
+    row_part = jnp.where(in_first_row, u_total + swap(u_total), v_total + swap(v_total))
+    refs.row[...] = row_part
+    u_sum, v_sum = refs.u_sum[...], refs.v_sum[...]
+    col_ref[:depth] = jnp.where(in_first, u_sum, swap(v_sum))
+    col_ref[depth:] = jnp.zeros((half, lanes), jnp.float32)
+    col_ref[half:] += jnp.where(in_first, swap(u_sum), v_sum)
+
+    away = lax.rem(owner + n_row - row, n_row) - 1
+
+    def owned_copy(d, target):
+        return remote(
+            col_ref, refs.from_owned.at[d], refs.send_e.at[0], refs.recv_e.at[d], target, col
+        )
+
+    @pl.when(row != owner)
+    def _():
+        owned_copy(away, owner).start()
+
     def predict(n, carry):
         out = jnp.dot(lay(n), weight_ref[...], preferred_element_type=jnp.float32)
         out = out.reshape(STEP, span, 3 * lanes)
@@ -290,6 +297,8 @@
     bins_back = to_all(bins_total, refs.bins_landing, back_sems, 0)
     taps_back = to_all(taps_total, refs.taps_landing, back_sems, n_col - 1)
 
+    some(0)
+
     @pl.when(row == owner)
     def _():
         mine = col_ref[...]
@@ -307,7 +316,6 @@
     taps_sum[chunk : chunk + STEP] = refs.row[:STEP]
     taps_sum[chunk + STEP : chunk + 2 * STEP] = refs.row[STEP + rows :]
     start(bins_out)
-    some(0)
     wait(to_row)
     mine = refs.packed[rows_at(row, chunk)]
     for d in range(n_row - 1):
@@ -419,6 +427,7 @@
         "act": pltpu.VMEM((blocks + 2, STEP * span, lanes), bf16),
         "turned": pltpu.VMEM((blocks, STEP * span, 3 * lanes), bf16),
         "grad": pltpu.VMEM((blocks + 2, STEP, span, lanes), f32),
+        "slope": pltpu.VMEM((blocks + 2, STEP, span, lanes), f32),
         "product": pltpu.VMEM((3 * lanes, 3 * lanes), f32),
         "u_sum": pltpu.VMEM((depth, lanes), f32),
         "v_sum": pltpu.VMEM((depth, lanes), f32),

time: 33.7 us -> 33.9 us (level)
  no operation moved by 1% of the time
where the time goes in v8:
time: 33.9 us; the launch traced here: 33.8 us
  Pallas kernels  33.1 us (98%)
  between operations  0.64 us (2%)
    pallas_call x1, Pallas kernels, on_device(): pl.pallas_call(tile, out_shape=tuple(outputs.values()), in_specs=[HBM, HB...  31.7 us
    pallas_call x1, Pallas kernels, on_device(): pl.pallas_call(functools.partial(finish_kernel, bins), out_shape=tuple(ou...  1.45 us

profile of v8, /device:TPU:0, one launch (start us, length us, event | category | flops | bytes accessed | tf_op | source)
XLA Modules:
  0.0 33.8 jit_solution(13314482325101570369)
XLA Ops:
  0.6 31.7 %tile_gradients.1 = (f32[64,64,128]{2,1,0:T(8,128)S(1)}, f32[576,64]{1,0:T(8,128)S(1)}, f32[128,128]{1,0:T(8,128)S(1)}) custom-call(bf16[128,128]{1,0:T(8,128)(2,1)} %refs_0_.1, bf16[3,3,64,64]{3,2,1,0:T(8,128)(2,1)} %refs_1_.1, bf16[64,64,128]{2,1,0:T(8,128)(2,1)} %bitcast.3), custom_call_target="tpu_custom_call" | custom-call | tf_op jit(solution)/shard_map/tile_gradients/pallas_call | solution.py:470
  32.3 1.4 %finish.1 = (f32[64,64,128]{2,1,0:T(8,128)}, f32[576,64]{1,0:T(8,128)}, f32[128,128]{1,0:T(8,128)}) custom-call(f32[64,64,128]{2,1,0:T(8,128)S(1)} %get-tuple-element.9.pred_in, f32[576,64]{1,0:T(8,128)S(1)} %get-tuple-element.10.taps_in, f32[128,128]{1,0:T(8,128)S(1)} %get-tuple-element.11.bins_in), custom_call_target="tpu_custom_call" | custom-call | tf_op jit(solution)/shard_map/finish/pallas_call | solution.py:482
